TPU v7x, 128 devices: a whole 4x4x4 slice. The times are simulated.
128 devices in a mesh: sample: 16 (over z_lo, x, core), tensor: 8 (over y, z_hi).
Axes of the slice: x: 4, y: 4, z: 4 (z_hi: 2, z_lo: 2; z = z_hi * 2 + z_lo), core: 2. Of those that a mesh axis runs over, the one named last changes fastest.
Arguments:
- branch_tokens: bfloat16 [4096, 8192], P('sample', 'tensor'), may hold values from -6 to 6
- norm_gain: bfloat16 [8192], replicated, may hold values from 0.099609375 to 1.8984375
- query_weight: bfloat16 [8192, 8192], P(None, 'tensor'), may hold values from -0.0625 to 0.0625
- key_weight: bfloat16 [8192, 1024], P(None, 'tensor'), may hold values from -0.21875 to 0.21875
- value_weight: bfloat16 [8192, 1024], P(None, 'tensor'), may hold values from -0.0625 to 0.0625
- kv_pool: bfloat16 [640, 2, 128, 1024], P('sample', None, None, 'tensor'), may hold values from -200 to 200
- parent_owner: int32 [128], replicated, may hold values from 0 to 15, as said below
- parent_pages: int32 [128], replicated, may hold values from 1 to 5
- page_table: int32 [128, 5], replicated, may hold values from 0 to 39, as said below
- child_parent: int32 [1024], replicated, may hold values from 0 to 127, as said below
Outputs:
- attn_out: bfloat16 [4096, 8192], P('sample', 'tensor')
Inputs may be any that keep to these rules, and one draw needn't show every extreme that they name: `parent_owner`: every index of sample holds the pages of exactly 8 parents. `page_table`: entries are pages of the owner's pool; all 5 entries of all parents of one owner are distinct. `child_parent`: every parent is named by exactly 8 children.
All inputs are finite; a program needn't handle non-finite values.
Results may differ from a plain program's by a relative error of at most 0.007.
The roundings to bfloat16 on the way count: a program that leaves them out, or rounds other values in their place, can miss the bound.
Values may be sent and summed in bfloat16 or wider, within the bound.
No kernel may reach another device: no remote copies, remote signals or barrier semaphores. Data moves between devices by JAX's collectives and lax.ppermute only.
A program may use at most 192 MiB of HBM per device.

v0:
```python
import math

import jax
import jax.numpy as jnp
from jax import lax
from jax.sharding import PartitionSpec as P

HEAD_SIZE = 128
PAGE_TOKENS = 128
CHILD_STEPS = 4


ROPE_THETA = 10000.0
EPSILON = 1e-06


def lookup(small_table, indices):
    matches = indices[:, None] == jnp.arange(small_table.shape[0], dtype=jnp.int32)[None, :]
    return jnp.sum(jnp.where(matches, small_table[None, :], 0), axis=1)


def norm_rows(tokens, gain_row):
    row_float = tokens.astype(jnp.float32)
    mean_square = jnp.mean(row_float * row_float, axis=1, keepdims=True)
    return (row_float * lax.rsqrt(mean_square + EPSILON) * gain_row.astype(jnp.float32)).astype(
        jnp.bfloat16
    )


def rotate(vectors, token_positions):
    half_width = vectors.shape[-1] // 2
    inverse_freq = ROPE_THETA ** (
        -2.0 * jnp.arange(half_width, dtype=jnp.float32) / vectors.shape[-1]
    )
    angles = token_positions[:, None] * inverse_freq[None, :]
    cosine_part = jnp.cos(angles)[:, None, :]
    sine_part = jnp.sin(angles)[:, None, :]
    front_half = vectors[..., :half_width]
    back_half = vectors[..., half_width:]
    return jnp.concatenate(
        [
            front_half * cosine_part - back_half * sine_part,
            back_half * cosine_part + front_half * sine_part,
        ],
        axis=-1,
    )


def project_heads(normalized_rows, weight, token_positions, head_count):
    projected = jnp.dot(normalized_rows, weight, preferred_element_type=jnp.float32).reshape(
        normalized_rows.shape[0], head_count, HEAD_SIZE
    )
    return rotate(projected, token_positions).astype(jnp.bfloat16)


def attend(scores, value_rows, einsum_form):
    top_score = jnp.max(scores, axis=-1)
    weights = jnp.exp(scores - top_score[..., None])
    weight_sum = jnp.sum(weights, axis=-1)
    weighted = jnp.einsum(
        einsum_form, weights.astype(jnp.bfloat16), value_rows, preferred_element_type=jnp.float32
    )
    return (weighted, weight_sum, top_score)


def path_part(query_rows, path_block, counts, score_scale):
    batch_rows = path_block.shape[0]
    page_count = path_block.shape[1]
    page_len = path_block.shape[3]
    kv_heads = query_rows.shape[2]
    head_width = query_rows.shape[4]
    path_keys = path_block[:, :, 0].reshape(batch_rows, page_count * page_len, kv_heads, head_width)
    path_values = path_block[:, :, 1].reshape(
        batch_rows, page_count * page_len, kv_heads, head_width
    )
    scores = (
        jnp.einsum("nsjgd,ntjd->nsjgt", query_rows, path_keys, preferred_element_type=jnp.float32)
        * score_scale
    )
    live_mask = (
        jnp.arange(page_count * page_len, dtype=jnp.int32)[None, :] < (counts * page_len)[:, None]
    )
    scores = jnp.where(live_mask[:, None, None, None, :], scores, -jnp.inf)
    return attend(scores, path_values, "nsjgt,ntjd->nsjgd")


def own_part(query_rows, child_keys, child_values, score_scale):
    steps_here = query_rows.shape[1]
    scores = (
        jnp.einsum("nsjgd,nujd->nsjgu", query_rows, child_keys, preferred_element_type=jnp.float32)
        * score_scale
    )
    causal = (
        jnp.arange(steps_here, dtype=jnp.int32)[:, None]
        >= jnp.arange(steps_here, dtype=jnp.int32)[None, :]
    )
    scores = jnp.where(causal[None, :, None, None, :], scores, -jnp.inf)
    return attend(scores, child_values, "nsjgu,nujd->nsjgd")


def combine(path_terms, own_terms):
    path_mix, path_total, path_top = path_terms
    own_mix, own_total, own_top = own_terms
    joint_top = jnp.maximum(path_top, own_top)
    path_factor = jnp.exp(path_top - joint_top)
    own_factor = jnp.exp(own_top - joint_top)
    numerator = path_mix * path_factor[..., None] + own_mix * own_factor[..., None]
    return numerator / (path_total * path_factor + own_total * own_factor)[..., None]


def local(
    branch_tokens,
    norm_gain,
    query_weight,
    key_weight,
    value_weight,
    kv_pool,
    parent_owner,
    parent_pages,
    page_table,
    child_parent,
):
    score_scale = 1.0 / math.sqrt(HEAD_SIZE)
    full_rows = lax.all_gather(branch_tokens, "tensor", axis=1, tiled=True)
    normalized_rows = norm_rows(full_rows, norm_gain)
    row_count = full_rows.shape[0]
    child_count = row_count // CHILD_STEPS
    kv_heads = key_weight.shape[1] // HEAD_SIZE
    query_group_count = query_weight.shape[1] // key_weight.shape[1]
    sample_index = lax.axis_index("sample")
    my_parents = lax.dynamic_slice_in_dim(child_parent, sample_index * child_count, child_count)
    my_counts = lookup(parent_pages, my_parents)
    token_positions = (
        jnp.repeat(my_counts * PAGE_TOKENS, CHILD_STEPS)
        + jnp.tile(jnp.arange(CHILD_STEPS, dtype=jnp.int32), child_count)
    ).astype(jnp.float32)
    query_rows = project_heads(
        normalized_rows, query_weight, token_positions, kv_heads * query_group_count
    ).reshape(child_count, CHILD_STEPS, kv_heads, query_group_count, HEAD_SIZE)
    child_keys = project_heads(normalized_rows, key_weight, token_positions, kv_heads).reshape(
        child_count, CHILD_STEPS, kv_heads, HEAD_SIZE
    )
    child_values = (
        jnp.dot(normalized_rows, value_weight, preferred_element_type=jnp.float32)
        .astype(jnp.bfloat16)
        .reshape(child_count, CHILD_STEPS, kv_heads, HEAD_SIZE)
    )
    every_page = lax.all_gather(kv_pool, "sample", axis=0, tiled=True)
    pool_size = kv_pool.shape[0]
    my_owners = lookup(parent_owner, my_parents)
    global_page_index = page_table[my_parents] + (my_owners * pool_size)[:, None]
    path_terms = path_part(query_rows, every_page[global_page_index], my_counts, score_scale)
    own_terms = own_part(query_rows, child_keys, child_values, score_scale)
    head_output = combine(path_terms, own_terms).astype(jnp.bfloat16)
    return head_output.reshape(row_count, kv_heads * query_group_count * HEAD_SIZE)


def solution(mesh):
    return jax.shard_map(
        local,
        mesh=mesh,
        in_specs=(
            P("sample", "tensor"),
            P(),
            P(None, "tensor"),
            P(None, "tensor"),
            P(None, "tensor"),
            P("sample", None, None, "tensor"),
            P(),
            P(),
            P(),
            P(),
        ),
        out_specs=P("sample", "tensor"),
        check_vma=False,
    )
```

profile of v0, /device:TPU:1, one launch (start us, length us, event | category | flops | bytes accessed | tf_op | source)
XLA Modules:
  0.0 361.9 jit_solution(12284532318120479814)
XLA Ops:
  6.5 0.0 copy-start
  6.5 0.0 all-gather.5.cloned.1.call-start
  6.5 0.7 all-gather.5.cloned.1.call-update
  7.3 0.0 all-gather.3.cloned.1.call-start
  7.3 0.7 all-gather.3.cloned.1.call-update
  8.0 0.7 convert_element_type.44
  8.7 0.8 compare_select_fusion.1
  9.5 0.8 select_reduce_fusion.1
  10.4 0.1 add_convert_fusion.1
  10.4 0.1 convert_element_type.47
  10.6 0.8 copy.41
  11.4 0.6 gather_fusion
  12.0 0.1 compare_select_fusion
  12.0 0.1 reshape.351
  12.2 0.1 iota_compare_fusion
  12.3 0.5 multiply_cosine_fusion
  12.9 71.3 %all-gather.5.cloned.1.call-done = bf16[256,8192]{1,0:T(8,128)(2,1)} async-done(((bf16[256,1024]{1,0:T(8,128)(2,1)}), bf16[256,8192]{1,0:T(8,128)(2,1)}) %all-gather.5.cloned.1.call-update) | async-done | bytes 4194320 | tf_op jit(solution)/shard_map/all_gather | solution.py:124
  84.2 3.1 fusion
  87.3 0.0 copy-start.2
  87.3 10.3 %convolution_bitcast_fusion = f32[32,8,8,128]{3,1,2,0:T(8,128)S(1)} fusion(bf16[8192,1024]{1,0:T(8,128)(2,1)} %param.12, bf16[256,8192]{1,0:T(8,128)(2,1)} %all-gather.5.cloned.1.call-done, f32[8192]{0:T(1024)S(1)} %convert_element_type.44, f32[256]{0:T(256)S(1)} %add_rsqrt_fusion), kind=kOutput, calls=%fused_computation.19 | convolution fusion | flops 4303355904 | bytes 22053888 | tf_op jit(solution)/shard_map/dot_general | solution.py:50
  97.5 0.2 copy.61
  97.8 0.0 copy-done
  97.8 0.0 copy-done.2
  97.8 1.7 convolution_bitcast_fusion.2
  99.5 0.3 fusion.42
  99.8 0.1 copy.45
  100.0 0.1 copy.44
  100.1 0.4 subtract_convert_fusion
  100.5 2.6 fusion.59
  103.1 0.1 copy.47
  103.2 0.5 fusion.31
  103.7 0.1 copy.53
  103.8 4.4 %convolution_convert_fusion = bf16[256,128]{1,0:T(8,128)(2,1)S(1)} fusion(bf16[8192,128]{1,0:T(8,128)(2,1)} %param.14, bf16[256,8192]{1,0:T(8,128)(2,1)} %all-gather.5.cloned.1.call-done, f32[8192]{0:T(1024)S(1)} %convert_element_type.44, f32[256]{0:T(256)S(1)} %add_rsqrt_fusion), kind=kOutput, calls=%fused_computation.30 | convolution fusion | flops 545292288 | bytes 6390784 | tf_op jit(solution)/shard_map/dot_general | solution.py:144
  108.2 186.4 %all-gather.3.cloned.1.call-done = bf16[640,2,128,128]{3,2,1,0:T(8,128)(2,1)} async-done(((bf16[40,2,128,128]{3,2,1,0:T(8,128)(2,1)}), bf16[640,2,128,128]{3,2,1,0:T(8,128)(2,1)}) %all-gather.3.cloned.1.call-update) | async-done | bytes 41943056 | tf_op jit(solution)/shard_map/all_gather | solution.py:148
  294.6 16.4 %gather_fusion.1 = bf16[320,2,128,128]{3,2,1,0:T(8,128)(2,1)} fusion(bf16[640,2,128,128]{3,2,1,0:T(8,128)(2,1)} %all-gather.3.cloned.1.call-done, s32[1024]{0:T(1024)S(1)} %pad_clamp_fusion), kind=kCustom, calls=%fused_computation.1 | custom fusion | bytes 41944320 | tf_op jit(solution)/shard_map/gather | solution.py:152
  311.0 19.3 %fusion.58 = (bf16[64,5,1,128,128]{4,3,2,1,0:T(8,128)(2,1)}, bf16[64,5,1,128,128]{4,3,2,1,0:T(8,128)(2,1)}) fusion(bf16[64,5,2,128,128]{4,3,2,1,0:T(8,128)(2,1)} %bitcast.136), kind=kLoop, calls=%fused_computation.81 | loop fusion | bytes 41943040 | tf_op jit(solution)/shard_map/slice | solution.py:73
  330.3 10.1 %bitcast_reduce_fusion = (f32[64,4,8]{2,1,0:T(4,128)S(1)}, f32[64,640,4,8]{1,3,2,0:T(8,128)}) fusion(pred[64,640]{1,0:T(8,128)(4,1)S(1)} %iota_compare_fusion, bf16[64,640,128,1]{2,1,3,0:T(8,128)(2,1)} %bitcast.137, bf16[64,4,8,64]{3,2,1,0:T(8,128)(2,1)S(1)} %bitcast.143, bf16[64,4,8,64]{3,2,1,0:T(8,128)(2,1)S(1)} %bitcast.141), kind=kOutput, calls=%fused_computation.8 | convolution fusion | flops 340523008 | bytes 16302080 | tf_op jit(solution)/shard_map/nsjgd,ntjd->nsjgt/dot_general | solution.py:77
  340.3 0.1 copy.48
  340.4 3.4 fusion.4
  343.8 0.1 copy.52
  343.9 0.1 copy.51
  344.0 0.1 copy.54
  344.1 0.1 copy.49
  344.2 1.6 fusion.25
  345.8 0.0 copy-start.1
  345.8 8.3 %fusion.26 = bf16[64,1,128,4,8]{2,4,3,0,1:T(8,128)(2,1)S(1)} fusion(f32[64,1,128,4,8]{2,4,3,0,1:T(8,128)} %fusion.25, bf16[64,640,128,1]{2,1,3,0:T(8,128)(2,1)} %bitcast.138, f32[64,640,4,8]{1,3,2,0:T(8,128)} %get-tuple-element.23, f32[64,4,8]{2,1,0:T(4,128)S(1)} %get-tuple-element.22, pred[64,640]{1,0:T(8,128)(4,1)S(1)} %iota_compare_fusion, ...), kind=kOutput, calls=%fused_computation.26 | convolution fusion | flops 341835776 | bytes 17367040 | tf_op jit(solution)/shard_map/nsjgt,ntjd->nsjgd/dot_general | solution.py:60
  354.1 0.9 copy.64
  355.0 0.0 copy-done.1
  (8 shorter events, 0.1 us)
Async XLA Ops:
  6.5 91.2 %copy-start = (bf16[8192,128]{1,0:T(8,128)(2,1)S(1)}, bf16[8192,128]{1,0:T(8,128)(2,1)}, u32[]{:S(2)}) copy-start(bf16[8192,128]{1,0:T(8,128)(2,1)} %param.13) | copy-start | bytes 6291460
  6.5 77.6 %all-gather.5.cloned.1.call-start = ((), (), s32[]{:S(2)}) async-start(), calls=%async_computation.1 | async-start | bytes 4718592 | tf_op jit(solution)/shard_map/all_gather | solution.py:124
  7.3 287.3 %all-gather.3.cloned.1.call-start = ((), (), s32[]{:S(2)}) async-start(), calls=%async_computation | async-start | bytes 44564480 | tf_op jit(solution)/shard_map/all_gather | solution.py:148
  87.3 10.5 %copy-start.2 = (bf16[256,8192]{1,0:T(8,128)(2,1)S(1)}, bf16[256,8192]{1,0:T(8,128)(2,1)}, u32[]{:S(2)}) copy-start(bf16[256,8192]{1,0:T(8,128)(2,1)} %all-gather.5.cloned.1.call-done) | copy-start | bytes 12582916
  345.8 9.2 %copy-start.1 = (bf16[8192,128]{1,0:T(8,128)(2,1)S(1)}, bf16[8192,128]{1,0:T(8,128)(2,1)}, u32[]{:S(2)}) copy-start(bf16[8192,128]{1,0:T(8,128)(2,1)} %param.13) | copy-start | bytes 6291460
Sparse Core Ops, SparseCore 0:
  9.7 74.3 all-gather.4
  85.9 208.6 all-gather.2
where the time goes:
time: 362 us
  waiting for transfers between devices  259 us (72%)
  local copies, waits for them, and re-layouts  39.3 us (11%)
  matrix products  39 us (11%)
  between operations  13.6 us (4%)
  other arithmetic  10.9 us (3%)
    all_gather x1, waiting for transfers between devices, local(): every_page = lax.all_gather(kv_pool, 'sample', axis=0, tiled=True)  186 us
    all_gather x1, waiting for transfers between devices, local(): full_rows = lax.all_gather(branch_tokens, 'tensor', axis=1, tiled=True)  71.3 us
    slice x1, local copies, waits for them, and re-layouts, path_part(): path_block[:, :, 1]  19.3 us
    gather x1, local copies, waits for them, and re-layouts, local(): every_page[global_page_index]  16.4 us
    dot_general x2, matrix products, project_heads(): jnp.dot(normalized_rows, weight, preferred_element_type=jnp.float32)  12 us
    dot_general x1, matrix products, path_part(): jnp.einsum('nsjgd,ntjd->nsjgt', query_rows, path_keys, preferred_element_...  10.1 us
    dot_general x2, matrix products, attend(): jnp.einsum(einsum_form, weights.astype(jnp.bfloat16), value_rows, preferr...  9.9 us
  transfers between devices with their start and end apart: 2, of which 2 were waited for; matrix products, arithmetic and copies ran while one was open for 8% of the time, Pallas kernels for 0%

commit v1 on v0

v1 whole, which is shorter than its diff:
```python
import functools
import math

import jax
import jax.numpy as jnp
from jax import lax
from jax.experimental import pallas as pl
from jax.experimental.pallas import tpu as pltpu
from jax.sharding import PartitionSpec as P

HEAD = 128
PAGE = 128
STEPS = 4
FORK = 8
PARENTS_HERE = 8
MOST_PAGES = 5
ROPE_THETA = 10000.0
EPSILON = 1e-06
SLOTS = 16

BF16 = jnp.bfloat16
F32 = jnp.float32


def iota(shape, dim):
    return lax.broadcasted_iota(jnp.int32, shape, dim)


def one(mask):
    return jnp.where(mask, 1.0, 0.0).astype(BF16)


def mm(a, b):
    return lax.dot_general(a, b, (((1,), (0,)), ((), ())), preferred_element_type=F32)


def mm_nt(a, b):
    return lax.dot_general(a, b, (((1,), (1,)), ((), ())), preferred_element_type=F32)


def mm_tn(a, b):
    return lax.dot_general(a, b, (((0,), (0,)), ((), ())), preferred_element_type=F32)


def route_kernel(
    slots,
    groups,
    me_ref,
    child_ref,
    owner_ref,
    pages_ref,
    table_ref,
    x_ref,
    send_ref,
    to_ref,
    from_ref,
    info_ref,
    count_ref,
):
    me = me_ref[0]
    children = child_ref.shape[1]
    parents = owner_ref.shape[1]
    rows = x_ref.shape[0]
    here = rows // STEPS
    child = child_ref[...]
    owner = owner_ref[...]
    parent_hot = one(iota((parents, children), 0) == child)
    owner_of = mm(jnp.broadcast_to(owner.astype(F32), (16, parents)).astype(BF16), parent_hot)[0:1]
    owner_mask = one(iota((groups, children), 0) == owner_of.astype(jnp.int32))
    per_home = mm(owner_mask, one(iota((children, 128), 0) // here == iota((children, 128), 1)))
    count_ref[0] = jnp.max(per_home).astype(jnp.int32)

    pick = one(iota((children, rows), 0) == me * here + iota((children, rows), 1) // STEPS)
    home_mask = mm(owner_mask, pick)
    before = one(
        (iota((rows, rows), 0) // STEPS < iota((rows, rows), 1) // STEPS)
        & (iota((rows, rows), 0) % STEPS == 0)
    )
    rank = mm(home_mask.astype(BF16), before)
    target = jnp.sum(
        home_mask * (iota((groups, rows), 0).astype(F32) * (slots * STEPS) + rank * STEPS),
        axis=0,
        keepdims=True,
    ).astype(jnp.int32) + iota((1, rows), 1) % STEPS
    to_hot = one(iota((groups * slots * STEPS, rows), 0) == target)
    to_ref[...] = to_hot
    send_ref[...] = mm(to_hot, x_ref[...]).astype(BF16)

    mine_parent = owner == me
    tri = one(iota((parents, parents), 0) < iota((parents, parents), 1))
    tri_home = one(
        (iota((128, 128), 0) < iota((128, 128), 1))
        & (iota((128, 128), 0) // here == iota((128, 128), 1) // here)
    )
    tri_block = one(iota((128, 128), 0) < iota((128, 128), 1))
    parent_rank = mm(one(jnp.broadcast_to(mine_parent, (16, parents))), tri)[0:1].astype(jnp.int32)
    mine_hot = (iota((PARENTS_HERE, parents), 0) == parent_rank) & mine_parent
    pages = jnp.sum(jnp.where(mine_hot, pages_ref[...], 0), axis=1, keepdims=True)
    mine_hot = one(mine_hot)
    table = mm(mine_hot, table_ref[...].astype(F32).astype(BF16)).astype(jnp.int32)
    info_ref[...] = jnp.where(iota((PARENTS_HERE, 8), 1) == MOST_PAGES, pages, table)
    member = mm(mine_hot, parent_hot)
    carry = jnp.zeros((PARENTS_HERE, 1), F32)
    places, spots = [], []
    for block in range(children // 128):
        part = member[:, block * 128 : (block + 1) * 128]
        ahead = mm(part.astype(BF16), tri_block) + carry
        carry = carry + jnp.sum(part, axis=1, keepdims=True)
        is_mine = jnp.sum(part, axis=0, keepdims=True)
        place = jnp.sum(
            part * (iota((PARENTS_HERE, 128), 0).astype(F32) * FORK + ahead), axis=0, keepdims=True
        )
        in_home = mm(jnp.broadcast_to(is_mine, (16, 128)).astype(BF16), tri_home)[0:1]
        home = (block * 128 + iota((1, 128), 1)) // here
        spot = home.astype(F32) * slots + in_home
        places.append(jnp.where(is_mine > 0.5, place, -1.0))
        spots.append(jnp.where(is_mine > 0.5, spot, -1.0))
    place = jnp.concatenate(places, axis=1).astype(jnp.int32)
    spot = jnp.concatenate(spots, axis=1).astype(jnp.int32)
    place_hot = one(iota((here, children), 0) == place)
    spot_hot = one(iota((groups * slots, children), 0) == spot)
    from_child = mm_nt(place_hot, spot_hot).astype(BF16)
    wide = groups * slots * STEPS
    grow_rows = one(iota((rows, here), 0) // STEPS == iota((rows, here), 1))
    grow_columns = one(
        iota((groups * slots, wide), 0) == iota((groups * slots, wide), 1) // STEPS
    )
    from_rows = mm(mm(grow_rows, from_child).astype(BF16), grow_columns)
    same_step = iota((rows, wide), 0) % STEPS == iota((rows, wide), 1) % STEPS
    from_ref[...] = jnp.where(same_step, from_rows, 0.0).astype(BF16)


def route(slots, groups, me, child_parent, parent_owner, parent_pages, page_table, rows):
    count, width = rows.shape
    wide = groups * slots * STEPS
    vmem = pl.BlockSpec(memory_space=pltpu.VMEM)
    smem = pl.BlockSpec(memory_space=pltpu.SMEM)
    return pl.pallas_call(
        functools.partial(route_kernel, slots, groups),
        out_shape=(
            jax.ShapeDtypeStruct((wide, width), BF16),
            jax.ShapeDtypeStruct((wide, count), BF16),
            jax.ShapeDtypeStruct((count, wide), BF16),
            jax.ShapeDtypeStruct((PARENTS_HERE, 8), jnp.int32),
            jax.ShapeDtypeStruct((1,), jnp.int32),
        ),
        in_specs=[smem] + [vmem] * 5,
        out_specs=(vmem, vmem, vmem, vmem, smem),
        compiler_params=pltpu.CompilerParams(vmem_limit_bytes=48 * 2**20),
    )(
        me,
        child_parent.reshape(1, -1),
        parent_owner.reshape(1, -1),
        parent_pages.reshape(1, -1),
        jnp.pad(page_table, ((0, 0), (0, 8 - page_table.shape[1]))),
        rows,
    )


def pick_kernel(hot_ref, rows_ref, out_ref):
    out_ref[...] = mm(hot_ref[...], rows_ref[...]).astype(BF16)


def pick_tn_kernel(hot_ref, rows_ref, out_ref):
    out_ref[...] = mm_tn(hot_ref[...], rows_ref[...]).astype(BF16)


def pick_rows(body, hot, rows, count):
    vmem = pl.BlockSpec(memory_space=pltpu.VMEM)
    return pl.pallas_call(
        body,
        out_shape=jax.ShapeDtypeStruct((count, rows.shape[1]), BF16),
        in_specs=[vmem, vmem],
        out_specs=vmem,
        compiler_params=pltpu.CompilerParams(vmem_limit_bytes=48 * 2**20),
    )(hot, rows)


def layer_kernel(
    width,
    order_ref,
    info_ref,
    *refs,
):
    blocks = refs[:8]
    (
        gain_ref,
        wq_ref,
        wk_ref,
        wv_ref,
        cos_ref,
        sin_ref,
        pool_ref,
        back_ref,
        out_ref,
        acc_q,
        acc_k,
        acc_v,
        scale_ref,
        x_ref,
        q_ref,
        k_ref,
        v_ref,
        o_ref,
    ) = refs[8:]
    step = pl.program_id(0)
    rows = blocks[0].shape[0]

    @pl.when(step == 0)
    def _():
        total = jnp.zeros((rows, 1), F32)
        for block in blocks:
            x = block[...].astype(F32)
            total = total + jnp.sum(x * x, axis=1, keepdims=True)
        scale_ref[...] = jnp.broadcast_to(
            lax.rsqrt(total * (1.0 / width) + EPSILON), scale_ref.shape
        )
        acc_q[...] = jnp.zeros_like(acc_q)
        acc_k[...] = jnp.zeros_like(acc_k)
        acc_v[...] = jnp.zeros_like(acc_v)

    for i, block in enumerate(blocks):

        @pl.when(step == i)
        def _(block=block):
            x = block[...].astype(F32) * scale_ref[:, 0:1] * gain_ref[0].astype(F32)
            x_ref[...] = x.astype(BF16)

    x = x_ref[...]
    acc_q[...] += mm(x, wq_ref[...])
    acc_k[...] += mm(x, wk_ref[...])
    acc_v[...] += mm(x, wv_ref[...])

    @pl.when(step == 7)
    def _():
        cos = cos_ref[...]
        sin = sin_ref[...]

        def turn(part):
            return (part * cos + pltpu.roll(part, HEAD // 2, 1) * sin).astype(BF16)

        heads = acc_q.shape[1] // HEAD
        for h in range(heads):
            cut = slice(h * HEAD, (h + 1) * HEAD)
            q_ref[:, cut] = turn(acc_q[:, cut])
        k_ref[...] = turn(acc_k[...])
        v_ref[...] = acc_v[...].astype(BF16)

        family = FORK * STEPS
        scale = 1.0 / math.sqrt(HEAD)
        row_at = iota((heads * family, family), 0) % family
        key_at = iota((heads * family, family), 1)
        own_mask = (row_at // STEPS == key_at // STEPS) & (row_at >= key_at)

        @pl.loop(0, PARENTS_HERE)
        def _(j):
            at = pl.ds(pl.multiple_of(j * family, family), family)
            q = jnp.concatenate(
                [q_ref[at, h * HEAD : (h + 1) * HEAD] for h in range(heads)], axis=0
            )
            own = jnp.where(own_mask, mm_nt(q, k_ref[at, :]) * scale, -jnp.inf)
            own_top = jnp.max(own, axis=1, keepdims=True)
            own_weight = jnp.exp(own - own_top)
            own_total = jnp.sum(own_weight, axis=1, keepdims=True)
            own_mix = mm(own_weight.astype(BF16), v_ref[at, :])
            length = info_ref[j, MOST_PAGES]
            for n in range(1, MOST_PAGES + 1):

                @pl.when(length == n)
                def _(n=n):
                    ids = [info_ref[j, i] for i in range(n)]
                    keys = jnp.concatenate([pool_ref[i, 0] for i in ids], axis=0)
                    values = jnp.concatenate([pool_ref[i, 1] for i in ids], axis=0)
                    path = mm_nt(q, keys) * scale
                    path_top = jnp.max(path, axis=1, keepdims=True)
                    weight = jnp.exp(path - path_top)
                    path_total = jnp.sum(weight, axis=1, keepdims=True)
                    path_mix = mm(weight.astype(BF16), values)
                    top = jnp.maximum(path_top, own_top)
                    path_factor = jnp.exp(path_top - top)
                    own_factor = jnp.exp(own_top - top)
                    both = path_mix * path_factor + own_mix * own_factor
                    out = both / (path_total * path_factor + own_total * own_factor)
                    out = out.astype(BF16)
                    for h in range(heads):
                        o_ref[at, h * HEAD : (h + 1) * HEAD] = out[h * family : (h + 1) * family]

        out_ref[...] = mm_tn(back_ref[...], o_ref[...]).astype(BF16)


def layer(order, info, blocks, gain, wq, wk, wv, cos, sin, pool, back):
    rows, part = blocks[0].shape
    width = wq.shape[0]
    wide = back.shape[1]

    def whole(a):
        return pl.BlockSpec(a.shape, lambda i, order, info: (0,) * a.ndim)

    return pl.pallas_call(
        functools.partial(layer_kernel, width),
        out_shape=jax.ShapeDtypeStruct((wide, wq.shape[1]), BF16),
        grid_spec=pltpu.PrefetchScalarGridSpec(
            num_scalar_prefetch=2,
            grid=(8,),
            in_specs=[whole(b) for b in blocks]
            + [pl.BlockSpec((1, 1, part), lambda i, order, info: (order[i], 0, 0))]
            + [
                pl.BlockSpec((part, w.shape[1]), lambda i, order, info: (order[i], 0))
                for w in (wq, wk, wv)
            ]
            + [whole(a) for a in (cos, sin, pool, back)],
            out_specs=pl.BlockSpec((wide, wq.shape[1]), lambda i, order, info: (0, 0)),
            scratch_shapes=[
                pltpu.VMEM((rows, wq.shape[1]), F32),
                pltpu.VMEM((rows, HEAD), F32),
                pltpu.VMEM((rows, HEAD), F32),
                pltpu.VMEM((rows, HEAD), F32),
                pltpu.VMEM((rows, part), BF16),
                pltpu.VMEM((rows, wq.shape[1]), BF16),
                pltpu.VMEM((rows, HEAD), BF16),
                pltpu.VMEM((rows, HEAD), BF16),
                pltpu.VMEM((rows, wq.shape[1]), BF16),
            ],
        ),
        compiler_params=pltpu.CompilerParams(
            vmem_limit_bytes=56 * 2**20, dimension_semantics=("arbitrary",)
        ),
    )(order, info, *blocks, gain.reshape(8, 1, part), wq, wk, wv, cos, sin, pool, back)


def moves(dy, dz):
    return [(t, ((t // 2 + dy) % 4) * 2 + (t + dz) % 2) for t in range(8)]


def gather_tensor(x):
    def shift(block, dy, dz):
        return lax.ppermute(block, "tensor", moves(dy, dz))

    found = {(0, 0): x}
    found[3, 0] = shift(x, 1, 0)
    found[1, 0] = shift(x, -1, 0)
    found[0, 1] = shift(x, 0, 1)
    found[2, 0] = shift(found[3, 0], 1, 0)
    found[1, 1] = shift(found[0, 1], -1, 0)
    found[3, 1] = shift(found[3, 0], 0, 1)
    half = x.shape[0] // 2
    low = shift(found[3, 1][:half], 1, 0)
    high = shift(found[1, 1][half:], -1, 0)
    found[2, 1] = jnp.concatenate([low, high], axis=0)
    return found


def after_route(slots, groups, arrays, routed):
    (norm_gain, query_weight, key_weight, value_weight, kv_pool) = arrays
    send, to_hot, from_hot, info = routed
    rows = from_hot.shape[0]
    wide, width = send.shape
    came = lax.all_to_all(send.reshape(groups, wide // groups, width), "sample", 0, 0)
    mine = pick_rows(pick_kernel, from_hot, came.reshape(wide, width), rows)
    found = gather_tensor(mine)
    keys = list(found)
    t = lax.axis_index("tensor")
    order = jnp.stack([((t // 2 + dy) % 4) * 2 + (t + dz) % 2 for dy, dz in keys]).astype(jnp.int32)
    pages = info[:, MOST_PAGES]
    positions = (
        jnp.repeat(pages * PAGE, FORK * STEPS)
        + jnp.tile(jnp.arange(STEPS, dtype=jnp.int32), PARENTS_HERE * FORK)
    ).astype(F32)
    half = HEAD // 2
    inverse = ROPE_THETA ** (-2.0 * jnp.arange(half, dtype=F32) / HEAD)
    angles = positions[:, None] * inverse[None, :]
    cos, sin = jnp.cos(angles), jnp.sin(angles)
    cos = jnp.concatenate([cos, cos], axis=1)
    sin = jnp.concatenate([-sin, sin], axis=1)
    back = layer(
        order,
        info,
        list(found.values()),
        norm_gain,
        query_weight,
        key_weight,
        value_weight,
        cos,
        sin,
        kv_pool,
        from_hot,
    )
    home = lax.all_to_all(back.reshape(groups, wide // groups, back.shape[1]), "sample", 0, 0)
    return pick_rows(pick_tn_kernel, to_hot, home.reshape(wide, back.shape[1]), rows)


def local(
    branch_tokens,
    norm_gain,
    query_weight,
    key_weight,
    value_weight,
    kv_pool,
    parent_owner,
    parent_pages,
    page_table,
    child_parent,
):
    groups = lax.axis_size("sample")
    me = lax.axis_index("sample").astype(jnp.int32).reshape(1)
    tables = (child_parent, parent_owner, parent_pages, page_table)
    arrays = (norm_gain, query_weight, key_weight, value_weight, kv_pool)
    *routed, most = route(SLOTS, groups, me, *tables, branch_tokens)

    def usual():
        return after_route(SLOTS, groups, arrays, routed)

    def crowded():
        slots = branch_tokens.shape[0] // STEPS
        *wider, _ = route(slots, groups, me, *tables, branch_tokens)
        return after_route(slots, groups, arrays, wider)

    return lax.cond(most[0] <= SLOTS, usual, crowded)


def solution(mesh):
    return jax.shard_map(
        local,
        mesh=mesh,
        in_specs=(
            P("sample", "tensor"),
            P(),
            P(None, "tensor"),
            P(None, "tensor"),
            P(None, "tensor"),
            P("sample", None, None, "tensor"),
            P(),
            P(),
            P(),
            P(),
        ),
        out_specs=P("sample", "tensor"),
        check_vma=False,
    )
```

time: 362 us -> 148 us (0.41)
  waiting for transfers between devices: 259 us -> 23.8 us
  blocking collectives: 0 us -> 67.2 us
  matrix products: 39 us -> 0 us
  local copies, waits for them, and re-layouts: 39.3 us -> 5.1 us
  Pallas kernels: 0 us -> 32 us
  starting transfers between devices: 0.04 us -> 15.2 us
  between operations: 13.6 us -> 0.7 us
  other arithmetic: 10.9 us -> 2.42 us
    all_gather x2 -> x0, waiting for transfers between devices: 258 us -> none  [the longest x1 186 us: local(): every_page = lax.all_gather(kv_pool, 'sample', axis=0, tiled=True)]
    all_to_all x0 -> x2, blocking collectives: none -> 67.2 us  [the longest x1 34 us: after_route(): lax.all_to_all(send.reshape(groups, wide // groups, width), 'sample', 0, 0)]
    dot_general x7 -> x0, matrix products: 39 us -> none  [the longest x2 12 us: project_heads(): jnp.dot(normalized_rows, weight, preferred_element_type=jnp.float32)]
    pallas_call x0 -> x4, Pallas kernels: none -> 32 us  [the longest x1 26.1 us: layer(): pl.pallas_call(functools.partial(layer_kernel, width), out_shape=jax.Shap...]
    ppermute x0 -> x8, waiting for transfers between devices: none -> 23.8 us  [shift(): return lax.ppermute(block, 'tensor', moves(dy, dz))]
    slice x1 -> x2, local copies, waits for them, and re-layouts: 19.3 us -> 1.93 us  [the longest x1 0.97 us: gather_tensor(): low = shift(found[3, 1][:half], 1, 0)]
    gather x2 -> x0, local copies, waits for them, and re-layouts: 17 us -> none  [the longest x1 16.4 us: local(): every_page[global_page_index]]
    ppermute x0 -> x8, starting transfers between devices: none -> 15.2 us  [shift(): return lax.ppermute(block, 'tensor', moves(dy, dz))]
  transfers between devices with their start and end apart: 2 -> 8, of which waited for: 2 -> 3; matrix products, arithmetic and copies ran while one was open for 8% -> 4% of each run, Pallas kernels for 0% -> 0%
where the time goes in v1:
time: 148 us; the launch traced here: 147 us
  blocking collectives  67.2 us (45%)
  Pallas kernels  32 us (22%)
  waiting for transfers between devices  23.8 us (16%)
  starting transfers between devices  15.2 us (10%)
  local copies, waits for them, and re-layouts  5.1 us (3%)
  other arithmetic  2.42 us (2%)
    all_to_all x1, blocking collectives, after_route(): lax.all_to_all(send.reshape(groups, wide // groups, width), 'sample', 0, 0)  34 us
    all_to_all x1, blocking collectives, after_route(): lax.all_to_all(back.reshape(groups, wide // groups, back.shape[1]), 'samp...  33.1 us
    pallas_call x1, Pallas kernels, layer(): pl.pallas_call(functools.partial(layer_kernel, width), out_shape=jax.Shap...  26.1 us
    ppermute x8, waiting for transfers between devices, shift(): return lax.ppermute(block, 'tensor', moves(dy, dz))  23.8 us
    ppermute x8, starting transfers between devices, shift(): return lax.ppermute(block, 'tensor', moves(dy, dz))  15.2 us
    pallas_call x1, Pallas kernels, route(): pl.pallas_call(functools.partial(route_kernel, slots, groups), out_shape=...  4.5 us
  transfers between devices with their start and end apart: 8, of which 3 were waited for; matrix products, arithmetic and copies ran while one was open for 4% of the time, Pallas kernels for 0%

profile of v1, /device:TPU:1, one launch (start us, length us, event | category | flops | bytes accessed | tf_op | source)
XLA Modules:
  0.0 146.6 jit_solution(4417097709958779633)
XLA Ops:
  0.0 0.8 copy.17
  0.8 4.5 %shard_map.102 = (bf16[1024,1024]{1,0:T(8,128)(2,1)}, bf16[1024,256]{1,0:T(8,128)(2,1)}, bf16[256,1024]{1,0:T(8,128)(2,1)}, s32[8,8]{1,0:T(8,128)S(1)}, s32[1]{0:T(128)}) custom-call(s32[1]{0:T(128)} %bitcast.27.me_ref, s32[1,1024]{1,0:T(1,128)} %bitcast.40, s32[1,128]{1,0:T(1,128)} %bitcast.42, s32[1,128]{1,0:T(1,128)} %bitcast.44, ...), custom_call_target="tpu_custom_call" | custom-call | tf_op jit(solution)/shard_map/pallas_call | solution.py:138
  6.0 139.8 %conditional.1 = (bf16[256,1024]{1,0:T(8,128)(2,1)S(1)}) conditional(s32[]{:T(128)} %bitcast.31, (s32[1024]{0:T(1024)}, s32[128]{0:T(128)}, s32[128]{0:T(128)}, s32[128,5]{0,1:T(8,128)}, s32[1]{0:T(128)}, /*index=5*/bf16[256,1024]{1,0:T(8,128)(2,1)}, bf16[8192]{0:T(1024)(128)(2,1)}, bf16[8192,1024]{1,0:T(8,128)(2,1)}, bf16[8192,128]{1,0:T(8,128)(2,1)}, ...), branch_computations={%region_0.1_spmd, %region_1.2_spmd} | conditional | flops 1147556 | bytes 88859200 | solution.py:418
  6.2 0.0 copy-start.8
  6.2 34.0 %all_to_all.18 = bf16[16,64,1024]{2,1,0:T(8,128)(2,1)S(1)} all-to-all(bf16[16,64,1024]{2,1,0:T(8,128)(2,1)} %bitcast.39), channel_id=1, replica_groups=mesh['sample'=16,'tensor'=8] {'sample'}, dimensions={0} | all-to-all | bytes 4194304 | tf_op jit(solution)/shard_map/cond/branch_1_fun/all_to_all | solution.py:358
  40.3 0.0 copy-start.13
  40.3 0.0 copy-done.8
  40.3 0.7 branch_1_fun.3.refs_0_
  41.0 0.0 copy-start.1
  41.0 0.0 copy-start.7
  41.0 3.4 %collective-permute-start.10 = (bf16[256,1024]{1,0:T(8,128)(2,1)S(1)}, bf16[256,1024]{1,0:T(8,128)(2,1)}, u32[]{:S(2)}, u32[]{:S(2)}) collective-permute-start(bf16[256,1024]{1,0:T(8,128)(2,1)S(1)} %branch_1_fun.3.refs_0_), channel_id=1, source_target_pairs={{0,1},{1,0},{2,3},{3,2},{4,5},{5,4},{6,7},{7,6},{8,9},{9,8},{10,11... | collective-permute-start | bytes 1572872 | tf_op jit(solution)/shard_map/cond/branch_1_fun/ppermute | solution.py:337
  44.4 1.3 collective-permute-start.8
  45.7 10.0 %collective-permute-done.10.refs_3_ = bf16[256,1024]{1,0:T(8,128)(2,1)} collective-permute-done((bf16[256,1024]{1,0:T(8,128)(2,1)S(1)}, bf16[256,1024]{1,0:T(8,128)(2,1)}, u32[]{:S(2)}, u32[]{:S(2)}) %collective-permute-start.10) | collective-permute-done | bytes 524320 | tf_op jit(solution)/shard_map/cond/branch_1_fun/ppermute | solution.py:337
  55.7 2.7 %collective-permute-start.12 = (bf16[256,1024]{1,0:T(8,128)(2,1)}, bf16[256,1024]{1,0:T(8,128)(2,1)}, u32[]{:S(2)}, u32[]{:S(2)}) collective-permute-start(bf16[256,1024]{1,0:T(8,128)(2,1)} %collective-permute-done.10.refs_3_), channel_id=1, source_target_pairs={{0,6},{1,7},{2,0},{3,1},{4,2},{5,3},{6,4},{7,5},{8,14},{9,15},{10,... | collective-permute-start | bytes 1572872 | tf_op jit(solution)/shard_map/cond/branch_1_fun/ppermute | solution.py:337
  58.4 0.0 collective-permute-done.8.refs_1_
  58.4 2.7 %collective-permute-start.13 = (bf16[256,1024]{1,0:T(8,128)(2,1)}, bf16[256,1024]{1,0:T(8,128)(2,1)}, u32[]{:S(2)}, u32[]{:S(2)}) collective-permute-start(bf16[256,1024]{1,0:T(8,128)(2,1)} %collective-permute-done.8.refs_1_), channel_id=1, source_target_pairs={{0,1},{1,0},{2,3},{3,2},{4,5},{5,4},{6,7},{7,6},{8,9},{9,8},{10,11... | collective-permute-start | bytes 1572872 | tf_op jit(solution)/shard_map/cond/branch_1_fun/ppermute | solution.py:337
  61.1 0.2 multiply_reduce_fusion.1
  61.3 0.1 broadcast_in_dim.6
  61.3 0.1 reshape.88
  61.4 0.1 tile.12
  61.6 0.5 collective-permute-start.9
  62.1 1.0 collective-permute-start.11
  63.1 0.0 copy-done.13
  63.1 0.6 reshape.101.refs_8_
  63.7 0.7 stack.53.order_ref
  64.4 0.0 copy-start.9
  64.4 3.9 %collective-permute-done.12.refs_5_ = bf16[256,1024]{1,0:T(8,128)(2,1)} collective-permute-done((bf16[256,1024]{1,0:T(8,128)(2,1)}, bf16[256,1024]{1,0:T(8,128)(2,1)}, u32[]{:S(2)}, u32[]{:S(2)}) %collective-permute-start.12) | collective-permute-done | bytes 524320 | tf_op jit(solution)/shard_map/cond/branch_1_fun/ppermute | solution.py:337
  68.3 1.0 slice.21
  69.3 3.5 %collective-permute-start.15 = (bf16[128,1024]{1,0:T(8,128)(2,1)S(1)}, bf16[128,1024]{1,0:T(8,128)(2,1)S(1)}, u32[]{:S(2)}, u32[]{:S(2)}) collective-permute-start(bf16[128,1024]{1,0:T(8,128)(2,1)S(1)} %slice.21), channel_id=1, source_target_pairs={{0,6},{1,7},{2,0},{3,1},{4,2},{5,3},{6,4},{7,5},{8,14},{9,15},{10,... | collective-permute-start | bytes 786440 | tf_op jit(solution)/shard_map/cond/branch_1_fun/ppermute | solution.py:337
  72.7 0.0 collective-permute-done.13.refs_6_
  72.7 1.0 slice.20
  73.7 0.1 collective-permute-start.14
  73.8 0.5 fusion.1
  74.3 0.9 pad_maximum_fusion.4
  75.2 9.8 %collective-permute-done.15 = bf16[128,1024]{1,0:T(8,128)(2,1)S(1)} collective-permute-done((bf16[128,1024]{1,0:T(8,128)(2,1)S(1)}, bf16[128,1024]{1,0:T(8,128)(2,1)S(1)}, u32[]{:S(2)}, u32[]{:S(2)}) %collective-permute-start.15) | collective-permute-done | bytes 262176 | tf_op jit(solution)/shard_map/cond/branch_1_fun/ppermute | solution.py:337
  85.0 0.0 collective-permute-done.14
  85.0 0.8 pad_maximum_fusion.3.refs_7_
  85.9 0.0 collective-permute-done.9.refs_2_
  85.9 0.0 collective-permute-done.11.refs_4_
  85.9 0.0 copy-done.1
  85.9 0.0 copy-done.7
  85.9 0.0 copy-done.9
  85.9 26.1 %branch_1_fun.4 = bf16[1024,1024]{1,0:T(8,128)(2,1)} custom-call(s32[8]{0:T(128)} %stack.53.order_ref, s32[8,8]{1,0:T(8,128)S(1)} %get-tuple-element.64.info_ref, bf16[256,1024]{1,0:T(8,128)(2,1)} %copy-done.1, bf16[256,1024]{1,0:T(8,128)(2,1)} %collective-permute-done.8.refs_1_, bf16[256,1024]{1,0:T(8,128)(2,1)} %collective-permute-done.9.refs_2_, ...), custom_call_target="tpu_custom_call" | custom-call | tf_op jit(solution)/shard_map/cond/branch_1_fun/pallas_call | solution.py:299
  112.0 0.0 copy-start.10
  112.0 33.1 %all_to_all.19 = bf16[16,64,1024]{2,1,0:T(8,128)(2,1)S(1)} all-to-all(bf16[16,64,1024]{2,1,0:T(8,128)(2,1)} %bitcast.37), channel_id=1, replica_groups=mesh['sample'=16,'tensor'=8] {'sample'}, dimensions={0} | all-to-all | bytes 4194304 | tf_op jit(solution)/shard_map/cond/branch_1_fun/all_to_all | solution.py:388
  145.1 0.0 copy-done.10
  145.1 0.7 branch_1_fun.5
  145.8 0.0 copy-start.11
  145.8 0.8 copy-done.11
  (4 shorter events, 0.0 us)
Async XLA Ops:
  6.2 34.1 %copy-start.8 = (bf16[256,1024]{1,0:T(8,128)(2,1)S(1)}, bf16[256,1024]{1,0:T(8,128)(2,1)}, u32[]{:S(2)}) copy-start(bf16[256,1024]{1,0:T(8,128)(2,1)} %get-tuple-element.65.hot_ref.refs_15_) | copy-start | bytes 1572868 | tf_op jit(solution)/shard_map/cond
  40.3 22.8 %copy-start.13 = (bf16[8192]{0:T(1024)(128)(2,1)S(1)}, bf16[8192]{0:T(1024)(128)(2,1)}, u32[]{:S(2)}) copy-start(bf16[8192]{0:T(1024)(128)(2,1)} %get-tuple-element.67) | copy-start | bytes 49156 | tf_op jit(solution)/shard_map/cond
  41.0 44.9 %copy-start.1 = (bf16[256,1024]{1,0:T(8,128)(2,1)}, bf16[256,1024]{1,0:T(8,128)(2,1)S(1)}, u32[]{:S(2)}) copy-start(bf16[256,1024]{1,0:T(8,128)(2,1)S(1)} %branch_1_fun.3.refs_0_) | copy-start | bytes 1572868 | tf_op jit(solution)/shard_map/cond
  41.0 44.9 %copy-start.7 = (bf16[40,2,128,128]{3,2,1,0:T(8,128)(2,1)S(1)}, bf16[40,2,128,128]{3,2,1,0:T(8,128)(2,1)}, u32[]{:S(2)}) copy-start(bf16[40,2,128,128]{3,2,1,0:T(8,128)(2,1)} %get-tuple-element.71.refs_14_) | copy-start | bytes 7864324 | tf_op jit(solution)/shard_map/cond
  41.0 14.7 %collective-permute-start.10 = (bf16[256,1024]{1,0:T(8,128)(2,1)S(1)}, bf16[256,1024]{1,0:T(8,128)(2,1)}, u32[]{:S(2)}, u32[]{:S(2)}) collective-permute-start(bf16[256,1024]{1,0:T(8,128)(2,1)S(1)} %branch_1_fun.3.refs_0_), channel_id=1, source_target_pairs={{0,1},{1,0},{2,3},{3,2},{4,5},{5,4},{6,7},{7,6},{8,9},{9,8},{10,11... | collective-permute-start | bytes 1572872 | tf_op jit(solution)/shard_map/cond/branch_1_fun/ppermute | solution.py:337
  44.4 14.0 %collective-permute-start.8 = (bf16[256,1024]{1,0:T(8,128)(2,1)S(1)}, bf16[256,1024]{1,0:T(8,128)(2,1)}, u32[]{:S(2)}, u32[]{:S(2)}) collective-permute-start(bf16[256,1024]{1,0:T(8,128)(2,1)S(1)} %branch_1_fun.3.refs_0_), channel_id=1, source_target_pairs={{0,2},{1,3},{2,4},{3,5},{4,6},{5,7},{6,0},{7,1},{8,10},{9,11},{10,... | collective-permute-start | bytes 1572872 | tf_op jit(solution)/shard_map/cond/branch_1_fun/ppermute | solution.py:337
  55.7 12.6 %collective-permute-start.12 = (bf16[256,1024]{1,0:T(8,128)(2,1)}, bf16[256,1024]{1,0:T(8,128)(2,1)}, u32[]{:S(2)}, u32[]{:S(2)}) collective-permute-start(bf16[256,1024]{1,0:T(8,128)(2,1)} %collective-permute-done.10.refs_3_), channel_id=1, source_target_pairs={{0,6},{1,7},{2,0},{3,1},{4,2},{5,3},{6,4},{7,5},{8,14},{9,15},{10,... | collective-permute-start | bytes 1572872 | tf_op jit(solution)/shard_map/cond/branch_1_fun/ppermute | solution.py:337
  58.4 14.3 %collective-permute-start.13 = (bf16[256,1024]{1,0:T(8,128)(2,1)}, bf16[256,1024]{1,0:T(8,128)(2,1)}, u32[]{:S(2)}, u32[]{:S(2)}) collective-permute-start(bf16[256,1024]{1,0:T(8,128)(2,1)} %collective-permute-done.8.refs_1_), channel_id=1, source_target_pairs={{0,1},{1,0},{2,3},{3,2},{4,5},{5,4},{6,7},{7,6},{8,9},{9,8},{10,11... | collective-permute-start | bytes 1572872 | tf_op jit(solution)/shard_map/cond/branch_1_fun/ppermute | solution.py:337
  61.6 24.3 %collective-permute-start.9 = (bf16[256,1024]{1,0:T(8,128)(2,1)S(1)}, bf16[256,1024]{1,0:T(8,128)(2,1)}, u32[]{:S(2)}, u32[]{:S(2)}) collective-permute-start(bf16[256,1024]{1,0:T(8,128)(2,1)S(1)} %branch_1_fun.3.refs_0_), channel_id=1, source_target_pairs={{0,6},{1,7},{2,0},{3,1},{4,2},{5,3},{6,4},{7,5},{8,14},{9,15},{10,... | collective-permute-start | bytes 1572872 | tf_op jit(solution)/shard_map/cond/branch_1_fun/ppermute | solution.py:337
  62.1 23.8 %collective-permute-start.11 = (bf16[256,1024]{1,0:T(8,128)(2,1)}, bf16[256,1024]{1,0:T(8,128)(2,1)}, u32[]{:S(2)}, u32[]{:S(2)}) collective-permute-start(bf16[256,1024]{1,0:T(8,128)(2,1)} %collective-permute-done.8.refs_1_), channel_id=1, source_target_pairs={{0,2},{1,3},{2,4},{3,5},{4,6},{5,7},{6,0},{7,1},{8,10},{9,11},{10,... | collective-permute-start | bytes 1572872 | tf_op jit(solution)/shard_map/cond/branch_1_fun/ppermute | solution.py:337
  64.4 21.5 %copy-start.9 = (bf16[256,1024]{1,0:T(8,128)(2,1)S(1)}, bf16[256,1024]{1,0:T(8,128)(2,1)}, u32[]{:S(2)}) copy-start(bf16[256,1024]{1,0:T(8,128)(2,1)} %get-tuple-element.65.hot_ref.refs_15_) | copy-start | bytes 1572868 | tf_op jit(solution)/shard_map/cond
  69.3 15.8 %collective-permute-start.15 = (bf16[128,1024]{1,0:T(8,128)(2,1)S(1)}, bf16[128,1024]{1,0:T(8,128)(2,1)S(1)}, u32[]{:S(2)}, u32[]{:S(2)}) collective-permute-start(bf16[128,1024]{1,0:T(8,128)(2,1)S(1)} %slice.21), channel_id=1, source_target_pairs={{0,6},{1,7},{2,0},{3,1},{4,2},{5,3},{6,4},{7,5},{8,14},{9,15},{10,... | collective-permute-start | bytes 786440 | tf_op jit(solution)/shard_map/cond/branch_1_fun/ppermute | solution.py:337
  73.7 11.3 %collective-permute-start.14 = (bf16[128,1024]{1,0:T(8,128)(2,1)S(1)}, bf16[128,1024]{1,0:T(8,128)(2,1)S(1)}, u32[]{:S(2)}, u32[]{:S(2)}) collective-permute-start(bf16[128,1024]{1,0:T(8,128)(2,1)S(1)} %slice.20), channel_id=1, source_target_pairs={{0,2},{1,3},{2,4},{3,5},{4,6},{5,7},{6,0},{7,1},{8,10},{9,11},{10,... | collective-permute-start | bytes 786440 | tf_op jit(solution)/shard_map/cond/branch_1_fun/ppermute | solution.py:337
  112.0 33.1 %copy-start.10 = (bf16[1024,256]{1,0:T(8,128)(2,1)S(1)}, bf16[1024,256]{1,0:T(8,128)(2,1)}, u32[]{:S(2)}) copy-start(bf16[1024,256]{1,0:T(8,128)(2,1)} %get-tuple-element.63.hot_ref) | copy-start | bytes 1572868 | tf_op jit(solution)/shard_map/cond
  145.8 0.8 copy-start.11

commit v2 on v1

--- a/solution.py
+++ b/solution.py
@@ -16,7 +16,7 @@
 MOST_PAGES = 5
 ROPE_THETA = 10000.0
 EPSILON = 1e-06
-SLOTS = 16
+SLOTS = 14
 
 BF16 = jnp.bfloat16
 F32 = jnp.float32
@@ -157,10 +157,6 @@
     )
 
 
-def pick_kernel(hot_ref, rows_ref, out_ref):
-    out_ref[...] = mm(hot_ref[...], rows_ref[...]).astype(BF16)
-
-
 def pick_tn_kernel(hot_ref, rows_ref, out_ref):
     out_ref[...] = mm_tn(hot_ref[...], rows_ref[...]).astype(BF16)
 
@@ -176,214 +172,281 @@
     )(hot, rows)
 
 
-def layer_kernel(
+def pick_sum_kernel(hot_ref, rows_ref, out_ref, sum_ref):
+    x = mm(hot_ref[...], rows_ref[...])
+    out_ref[...] = x.astype(BF16)
+    total = jnp.sum(x * x, axis=1, keepdims=True)
+    total = jnp.broadcast_to(total, (total.shape[0], 128)).T
+    sum_ref[...] = jnp.broadcast_to(total[0:1], sum_ref.shape[:1] + total.shape[1:])[:, None, :]
+
+
+def pick_and_sum(hot, rows, copies):
+    vmem = pl.BlockSpec(memory_space=pltpu.VMEM)
+    count = hot.shape[0]
+    return pl.pallas_call(
+        pick_sum_kernel,
+        out_shape=(
+            jax.ShapeDtypeStruct((count, rows.shape[1]), BF16),
+            jax.ShapeDtypeStruct((copies, 1, count), F32),
+        ),
+        in_specs=[vmem, vmem],
+        out_specs=(vmem, vmem),
+        compiler_params=pltpu.CompilerParams(vmem_limit_bytes=48 * 2**20),
+    )(hot, rows)
+
+
+def row_scale(sum_ref, width):
+    total = jnp.sum(sum_ref[:, 0, :], axis=0, keepdims=True)
+    scale = lax.rsqrt(total * (1.0 / width) + EPSILON)
+    return jnp.broadcast_to(scale, (128, scale.shape[1])).T
+
+
+def normed(x, scale, gain):
+    return (x.astype(F32) * scale * gain.astype(F32)).astype(BF16)
+
+
+def add_products(acc, x, wq_ref, wk_ref, wv_ref, wkv_ref):
+    wide = wq_ref.shape[1]
+    wkv_ref[:, :HEAD] = wk_ref[...]
+    wkv_ref[:, HEAD:] = wv_ref[...]
+    acc[:, :wide] += mm(x, wq_ref[...])
+    acc[:, wide:] += mm(x, wkv_ref[...])
+
+
+def project_kernel(width, count, first, order_ref, sum_ref, *refs):
+    blocks = refs[:count]
+    gain_ref, wq_ref, wk_ref, wv_ref = refs[count : count + 4]
+    before = None if first else refs[count + 4]
+    acc_ref, x_ref, scale_ref, wkv_ref = refs[-4:]
+    step = pl.program_id(0)
+
+    @pl.when(step == 0)
+    def _():
+        scale_ref[...] = row_scale(sum_ref, width)
+        acc_ref[...] = jnp.zeros_like(acc_ref) if first else before[...]
+
+    for i, block in enumerate(blocks):
+
+        @pl.when(step == i)
+        def _(block=block):
+            x_ref[...] = normed(block[...], scale_ref[:, 0:1], gain_ref[0])
+
+    add_products(acc_ref, x_ref[...], wq_ref, wk_ref, wv_ref, wkv_ref)
+
+
+def project(order, sums, blocks, gain, wq, wk, wv, before=None):
+    rows, part = blocks[0].shape
+    columns = wq.shape[1] + wk.shape[1] + wv.shape[1]
+    count = len(blocks)
+
+    def whole(a):
+        return pl.BlockSpec(a.shape, lambda i, order: (0,) * a.ndim)
+
+    extra = [] if before is None else [before]
+    return pl.pallas_call(
+        functools.partial(project_kernel, wq.shape[0], count, before is None),
+        out_shape=jax.ShapeDtypeStruct((rows, columns), F32),
+        grid_spec=pltpu.PrefetchScalarGridSpec(
+            num_scalar_prefetch=1,
+            grid=(count,),
+            in_specs=[whole(sums)]
+            + [whole(b) for b in blocks]
+            + [pl.BlockSpec((1, 1, part), lambda i, order: (order[i], 0, 0))]
+            + [
+                pl.BlockSpec((part, w.shape[1]), lambda i, order: (order[i], 0))
+                for w in (wq, wk, wv)
+            ]
+            + [whole(a) for a in extra],
+            out_specs=pl.BlockSpec((rows, columns), lambda i, order: (0, 0)),
+            scratch_shapes=[
+                pltpu.VMEM((rows, part), BF16),
+                pltpu.VMEM((rows, 128), F32),
+                pltpu.VMEM((part, 2 * HEAD), BF16),
+            ],
+        ),
+        compiler_params=pltpu.CompilerParams(vmem_limit_bytes=32 * 2**20),
+        cost_estimate=pl.CostEstimate(
+            flops=2 * rows * part * count * columns * 3,
+            bytes_accessed=2 * part * count * columns,
+            transcendentals=0,
+        ),
+    )(order, sums, *blocks, gain, wq, wk, wv, *extra)
+
+
+def attend_kernel(
     width,
     order_ref,
     info_ref,
-    *refs,
+    sum_ref,
+    low_ref,
+    high_ref,
+    gain_ref,
+    wq_ref,
+    wk_ref,
+    wv_ref,
+    before_ref,
+    cos_ref,
+    sin_ref,
+    pool_ref,
+    back_ref,
+    out_ref,
+    acc_ref,
+    x_ref,
+    wkv_ref,
+    q_ref,
+    k_ref,
+    v_ref,
+    o_ref,
 ):
-    blocks = refs[:8]
-    (
-        gain_ref,
-        wq_ref,
-        wk_ref,
-        wv_ref,
-        cos_ref,
-        sin_ref,
-        pool_ref,
-        back_ref,
-        out_ref,
-        acc_q,
-        acc_k,
-        acc_v,
-        scale_ref,
-        x_ref,
-        q_ref,
-        k_ref,
-        v_ref,
-        o_ref,
-    ) = refs[8:]
-    step = pl.program_id(0)
-    rows = blocks[0].shape[0]
-
-    @pl.when(step == 0)
-    def _():
-        total = jnp.zeros((rows, 1), F32)
-        for block in blocks:
-            x = block[...].astype(F32)
-            total = total + jnp.sum(x * x, axis=1, keepdims=True)
-        scale_ref[...] = jnp.broadcast_to(
-            lax.rsqrt(total * (1.0 / width) + EPSILON), scale_ref.shape
-        )
-        acc_q[...] = jnp.zeros_like(acc_q)
-        acc_k[...] = jnp.zeros_like(acc_k)
-        acc_v[...] = jnp.zeros_like(acc_v)
-
-    for i, block in enumerate(blocks):
-
-        @pl.when(step == i)
-        def _(block=block):
-            x = block[...].astype(F32) * scale_ref[:, 0:1] * gain_ref[0].astype(F32)
-            x_ref[...] = x.astype(BF16)
-
-    x = x_ref[...]
-    acc_q[...] += mm(x, wq_ref[...])
-    acc_k[...] += mm(x, wk_ref[...])
-    acc_v[...] += mm(x, wv_ref[...])
-
-    @pl.when(step == 7)
-    def _():
-        cos = cos_ref[...]
-        sin = sin_ref[...]
-
-        def turn(part):
-            return (part * cos + pltpu.roll(part, HEAD // 2, 1) * sin).astype(BF16)
-
-        heads = acc_q.shape[1] // HEAD
-        for h in range(heads):
-            cut = slice(h * HEAD, (h + 1) * HEAD)
-            q_ref[:, cut] = turn(acc_q[:, cut])
-        k_ref[...] = turn(acc_k[...])
-        v_ref[...] = acc_v[...].astype(BF16)
-
-        family = FORK * STEPS
-        scale = 1.0 / math.sqrt(HEAD)
-        row_at = iota((heads * family, family), 0) % family
-        key_at = iota((heads * family, family), 1)
-        own_mask = (row_at // STEPS == key_at // STEPS) & (row_at >= key_at)
-
-        @pl.loop(0, PARENTS_HERE)
-        def _(j):
-            at = pl.ds(pl.multiple_of(j * family, family), family)
-            q = jnp.concatenate(
-                [q_ref[at, h * HEAD : (h + 1) * HEAD] for h in range(heads)], axis=0
-            )
-            own = jnp.where(own_mask, mm_nt(q, k_ref[at, :]) * scale, -jnp.inf)
-            own_top = jnp.max(own, axis=1, keepdims=True)
-            own_weight = jnp.exp(own - own_top)
-            own_total = jnp.sum(own_weight, axis=1, keepdims=True)
-            own_mix = mm(own_weight.astype(BF16), v_ref[at, :])
-            length = info_ref[j, MOST_PAGES]
-            for n in range(1, MOST_PAGES + 1):
-
-                @pl.when(length == n)
-                def _(n=n):
-                    ids = [info_ref[j, i] for i in range(n)]
-                    keys = jnp.concatenate([pool_ref[i, 0] for i in ids], axis=0)
-                    values = jnp.concatenate([pool_ref[i, 1] for i in ids], axis=0)
-                    path = mm_nt(q, keys) * scale
-                    path_top = jnp.max(path, axis=1, keepdims=True)
-                    weight = jnp.exp(path - path_top)
-                    path_total = jnp.sum(weight, axis=1, keepdims=True)
-                    path_mix = mm(weight.astype(BF16), values)
-                    top = jnp.maximum(path_top, own_top)
-                    path_factor = jnp.exp(path_top - top)
-                    own_factor = jnp.exp(own_top - top)
-                    both = path_mix * path_factor + own_mix * own_factor
-                    out = both / (path_total * path_factor + own_total * own_factor)
-                    out = out.astype(BF16)
-                    for h in range(heads):
-                        o_ref[at, h * HEAD : (h + 1) * HEAD] = out[h * family : (h + 1) * family]
-
-        out_ref[...] = mm_tn(back_ref[...], o_ref[...]).astype(BF16)
-
-
-def layer(order, info, blocks, gain, wq, wk, wv, cos, sin, pool, back):
-    rows, part = blocks[0].shape
-    width = wq.shape[0]
+    scale = row_scale(sum_ref, width)[:, 0:1]
+    half = low_ref.shape[0]
+    x_ref[:half] = normed(low_ref[...], scale[:half], gain_ref[0])
+    x_ref[half:] = normed(high_ref[...], scale[half:], gain_ref[0])
+    acc_ref[...] = before_ref[...]
+    add_products(acc_ref, x_ref[...], wq_ref, wk_ref, wv_ref, wkv_ref)
+
+    cos = cos_ref[...]
+    sin = sin_ref[...]
+
+    def turn(part):
+        return (part * cos + pltpu.roll(part, HEAD // 2, 1) * sin).astype(BF16)
+
+    heads = wq_ref.shape[1] // HEAD
+    for h in range(heads):
+        cut = slice(h * HEAD, (h + 1) * HEAD)
+        q_ref[:, cut] = turn(acc_ref[:, cut])
+    k_ref[...] = turn(acc_ref[:, heads * HEAD : (heads + 1) * HEAD])
+    v_ref[...] = acc_ref[:, (heads + 1) * HEAD :].astype(BF16)
+
+    family = FORK * STEPS
+    scale = 1.0 / math.sqrt(HEAD)
+    row_at = iota((heads * family, family), 0) % family
+    key_at = iota((heads * family, family), 1)
+    own_mask = (row_at // STEPS == key_at // STEPS) & (row_at >= key_at)
+
+    @pl.loop(0, PARENTS_HERE)
+    def _(j):
+        at = pl.ds(pl.multiple_of(j * family, family), family)
+        q = jnp.concatenate([q_ref[at, h * HEAD : (h + 1) * HEAD] for h in range(heads)], axis=0)
+        own = jnp.where(own_mask, mm_nt(q, k_ref[at, :]) * scale, -jnp.inf)
+        own_top = jnp.max(own, axis=1, keepdims=True)
+        own_weight = jnp.exp(own - own_top)
+        own_total = jnp.sum(own_weight, axis=1, keepdims=True)
+        own_mix = mm(own_weight.astype(BF16), v_ref[at, :])
+        length = info_ref[j, MOST_PAGES]
+        for n in range(1, MOST_PAGES + 1):
+
+            @pl.when(length == n)
+            def _(n=n):
+                ids = [info_ref[j, i] for i in range(n)]
+                keys = jnp.concatenate([pool_ref[i, 0] for i in ids], axis=0)
+                values = jnp.concatenate([pool_ref[i, 1] for i in ids], axis=0)
+                path = mm_nt(q, keys) * scale
+                path_top = jnp.max(path, axis=1, keepdims=True)
+                weight = jnp.exp(path - path_top)
+                path_total = jnp.sum(weight, axis=1, keepdims=True)
+                path_mix = mm(weight.astype(BF16), values)
+                top = jnp.maximum(path_top, own_top)
+                path_factor = jnp.exp(path_top - top)
+                own_factor = jnp.exp(own_top - top)
+                both = path_mix * path_factor + own_mix * own_factor
+                out = both / (path_total * path_factor + own_total * own_factor)
+                out = out.astype(BF16)
+                for h in range(heads):
+                    o_ref[at, h * HEAD : (h + 1) * HEAD] = out[h * family : (h + 1) * family]
+
+    out_ref[...] = mm_tn(back_ref[...], o_ref[...]).astype(BF16)
+
+
+def attend(order, info, sums, low, high, gain, wq, wk, wv, before, cos, sin, pool, back):
+    rows, columns = before.shape
+    part = low.shape[1]
     wide = back.shape[1]
 
     def whole(a):
         return pl.BlockSpec(a.shape, lambda i, order, info: (0,) * a.ndim)
 
     return pl.pallas_call(
-        functools.partial(layer_kernel, width),
+        functools.partial(attend_kernel, wq.shape[0]),
         out_shape=jax.ShapeDtypeStruct((wide, wq.shape[1]), BF16),
         grid_spec=pltpu.PrefetchScalarGridSpec(
             num_scalar_prefetch=2,
-            grid=(8,),
-            in_specs=[whole(b) for b in blocks]
-            + [pl.BlockSpec((1, 1, part), lambda i, order, info: (order[i], 0, 0))]
+            grid=(1,),
+            in_specs=[whole(a) for a in (sums, low, high)]
+            + [pl.BlockSpec((1, 1, part), lambda i, order, info: (order[0], 0, 0))]
             + [
-                pl.BlockSpec((part, w.shape[1]), lambda i, order, info: (order[i], 0))
+                pl.BlockSpec((part, w.shape[1]), lambda i, order, info: (order[0], 0))
                 for w in (wq, wk, wv)
             ]
-            + [whole(a) for a in (cos, sin, pool, back)],
+            + [whole(a) for a in (before, cos, sin, pool, back)],
             out_specs=pl.BlockSpec((wide, wq.shape[1]), lambda i, order, info: (0, 0)),
             scratch_shapes=[
-                pltpu.VMEM((rows, wq.shape[1]), F32),
-                pltpu.VMEM((rows, HEAD), F32),
-                pltpu.VMEM((rows, HEAD), F32),
-                pltpu.VMEM((rows, HEAD), F32),
+                pltpu.VMEM((rows, columns), F32),
                 pltpu.VMEM((rows, part), BF16),
+                pltpu.VMEM((part, 2 * HEAD), BF16),
                 pltpu.VMEM((rows, wq.shape[1]), BF16),
                 pltpu.VMEM((rows, HEAD), BF16),
                 pltpu.VMEM((rows, HEAD), BF16),
                 pltpu.VMEM((rows, wq.shape[1]), BF16),
             ],
         ),
-        compiler_params=pltpu.CompilerParams(
-            vmem_limit_bytes=56 * 2**20, dimension_semantics=("arbitrary",)
-        ),
-    )(order, info, *blocks, gain.reshape(8, 1, part), wq, wk, wv, cos, sin, pool, back)
+        compiler_params=pltpu.CompilerParams(vmem_limit_bytes=48 * 2**20),
+        cost_estimate=pl.CostEstimate(
+            flops=2 * rows * part * columns * 6, bytes_accessed=2 * part * columns, transcendentals=0
+        ),
+    )(order, info, sums, low, high, gain, wq, wk, wv, before, cos, sin, pool, back)
 
 
 def moves(dy, dz):
     return [(t, ((t // 2 + dy) % 4) * 2 + (t + dz) % 2) for t in range(8)]
 
 
-def gather_tensor(x):
-    def shift(block, dy, dz):
-        return lax.ppermute(block, "tensor", moves(dy, dz))
-
-    found = {(0, 0): x}
-    found[3, 0] = shift(x, 1, 0)
-    found[1, 0] = shift(x, -1, 0)
-    found[0, 1] = shift(x, 0, 1)
-    found[2, 0] = shift(found[3, 0], 1, 0)
-    found[1, 1] = shift(found[0, 1], -1, 0)
-    found[3, 1] = shift(found[3, 0], 0, 1)
-    half = x.shape[0] // 2
-    low = shift(found[3, 1][:half], 1, 0)
-    high = shift(found[1, 1][half:], -1, 0)
-    found[2, 1] = jnp.concatenate([low, high], axis=0)
-    return found
-
-
 def after_route(slots, groups, arrays, routed):
-    (norm_gain, query_weight, key_weight, value_weight, kv_pool) = arrays
+    (norm_gain, wq, wk, wv, kv_pool) = arrays
     send, to_hot, from_hot, info = routed
     rows = from_hot.shape[0]
     wide, width = send.shape
+    team = lax.axis_size("tensor")
     came = lax.all_to_all(send.reshape(groups, wide // groups, width), "sample", 0, 0)
-    mine = pick_rows(pick_kernel, from_hot, came.reshape(wide, width), rows)
-    found = gather_tensor(mine)
-    keys = list(found)
+    mine, sums = pick_and_sum(from_hot, came.reshape(wide, width), team)
+
+    def shift(block, dy, dz):
+        return lax.ppermute(block, "tensor", moves(dy, dz))
+
     t = lax.axis_index("tensor")
-    order = jnp.stack([((t // 2 + dy) % 4) * 2 + (t + dz) % 2 for dy, dz in keys]).astype(jnp.int32)
+
+    def order(*keys):
+        places = [((t // 2 + dy) % 4) * 2 + (t + dz) % 2 for dy, dz in keys]
+        return jnp.stack(places).astype(jnp.int32)
+
+    gain = norm_gain.reshape(team, 1, -1)
+
+    sums = lax.all_to_all(sums, "tensor", 0, 0)
+    b30, b10, b01, sums = lax.optimization_barrier(
+        (shift(mine, 1, 0), shift(mine, -1, 0), shift(mine, 0, 1), sums)
+    )
+    second = (shift(b30, 1, 0), shift(b01, -1, 0), shift(b30, 0, 1))
+    acc = project(
+        order((0, 0), (3, 0), (1, 0), (0, 1)), sums, [mine, b30, b10, b01], gain, wq, wk, wv
+    )
+    b20, b11, b31, acc = lax.optimization_barrier((*second, acc))
+    half = rows // 2
+    low, high = shift(b31[:half], 1, 0), shift(b11[half:], -1, 0)
+    acc = project(order((2, 0), (1, 1), (3, 1)), sums, [b20, b11, b31], gain, wq, wk, wv, acc)
+    low, high, acc = lax.optimization_barrier((low, high, acc))
+
     pages = info[:, MOST_PAGES]
     positions = (
         jnp.repeat(pages * PAGE, FORK * STEPS)
         + jnp.tile(jnp.arange(STEPS, dtype=jnp.int32), PARENTS_HERE * FORK)
     ).astype(F32)
-    half = HEAD // 2
-    inverse = ROPE_THETA ** (-2.0 * jnp.arange(half, dtype=F32) / HEAD)
+    inverse = ROPE_THETA ** (-2.0 * jnp.arange(HEAD // 2, dtype=F32) / HEAD)
     angles = positions[:, None] * inverse[None, :]
     cos, sin = jnp.cos(angles), jnp.sin(angles)
     cos = jnp.concatenate([cos, cos], axis=1)
     sin = jnp.concatenate([-sin, sin], axis=1)
-    back = layer(
-        order,
-        info,
-        list(found.values()),
-        norm_gain,
-        query_weight,
-        key_weight,
-        value_weight,
-        cos,
-        sin,
-        kv_pool,
-        from_hot,
+    back = attend(
+        order((2, 1)), info, sums, low, high, gain, wq, wk, wv, acc, cos, sin, kv_pool, from_hot
     )
     home = lax.all_to_all(back.reshape(groups, wide // groups, back.shape[1]), "sample", 0, 0)
     return pick_rows(pick_tn_kernel, to_hot, home.reshape(wide, back.shape[1]), rows)

time: 148 us -> 125 us (0.84)
  blocking collectives: 67.2 us -> 32.3 us
  starting transfers between devices: 15.2 us -> 24.8 us
  waiting for transfers between devices: 23.8 us -> 32.1 us
  local copies, waits for them, and re-layouts: 5.1 us -> 1.93 us
    all_to_all x1 -> x0, blocking collectives: 34 us -> none  [after_route(): lax.all_to_all(send.reshape(groups, wide // groups, width), 'sample', 0, 0)]
    all_to_all x0 -> x2, waiting for transfers between devices: none -> 31.6 us  [the longest x1 23.8 us: after_route(): lax.all_to_all(send.reshape(groups, wide // groups, width), 'sample', 0, 0)]
    ppermute x8, waiting for transfers between devices: 23.8 us -> 0.53 us  [shift(): return lax.ppermute(block, 'tensor', moves(dy, dz))]
    all_to_all x0 -> x2, starting transfers between devices: none -> 10.6 us  [the longest x1 7.31 us: after_route(): lax.all_to_all(send.reshape(groups, wide // groups, width), 'sample', 0, 0)]
    slice x2, local copies, waits for them, and re-layouts: 1.93 us -> 0.04 us  [after_route(): low, high = (shift(b31[:half], 1, 0), shift(b11[half:], -1, 0))]
    pallas_call x1 -> x4, Pallas kernels: 26.1 us -> 26.1 us  [the longest x2 14 us: project(): pl.pallas_call(functools.partial(project_kernel, wq.shape[0], count, befo...]
  transfers between devices with their start and end apart: 8 -> 10, of which waited for: 3 -> 4; matrix products, arithmetic and copies ran while one was open for 4% -> 1% of each run, Pallas kernels for 0% -> 11%
where the time goes in v2:
time: 125 us; the launch traced here: 124 us
  blocking collectives  32.3 us (26%)
  waiting for transfers between devices  32.1 us (26%)
  Pallas kernels  31.1 us (25%)
  starting transfers between devices  24.8 us (20%)
  local copies, waits for them, and re-layouts  1.93 us (2%)
    all_to_all x1, blocking collectives, after_route(): lax.all_to_all(back.reshape(groups, wide // groups, back.shape[1]), 'samp...  32.3 us
    all_to_all x1, waiting for transfers between devices, after_route(): lax.all_to_all(send.reshape(groups, wide // groups, width), 'sample', 0, 0)  23.8 us
    ppermute x8, starting transfers between devices, shift(): return lax.ppermute(block, 'tensor', moves(dy, dz))  14.2 us
    pallas_call x2, Pallas kernels, project(): pl.pallas_call(functools.partial(project_kernel, wq.shape[0], count, befo...  14 us
    pallas_call x1, Pallas kernels, attend(): pl.pallas_call(functools.partial(attend_kernel, wq.shape[0]), out_shape=j...  10.6 us
    all_to_all x1, waiting for transfers between devices, after_route(): sums = lax.all_to_all(sums, 'tensor', 0, 0)  7.81 us
    all_to_all x1, starting transfers between devices, after_route(): lax.all_to_all(send.reshape(groups, wide // groups, width), 'sample', 0, 0)  7.31 us
    pallas_call x1, Pallas kernels, route(): pl.pallas_call(functools.partial(route_kernel, slots, groups), out_shape=...  4.33 us
  transfers between devices with their start and end apart: 10, of which 4 were waited for; matrix products, arithmetic and copies ran while one was open for 1% of the time, Pallas kernels for 11%

profile of v2, /device:TPU:1, one launch (start us, length us, event | category | flops | bytes accessed | tf_op | source)
XLA Modules:
  0.0 124.4 jit_solution(5718236747250907606)
XLA Ops:
  0.0 0.8 copy.21
  0.8 4.3 %shard_map.102 = (bf16[896,1024]{1,0:T(8,128)(2,1)}, bf16[896,256]{1,0:T(8,128)(2,1)}, bf16[256,896]{1,0:T(8,128)(2,1)}, s32[8,8]{1,0:T(8,128)S(1)}, s32[1]{0:T(128)}) custom-call(s32[1]{0:T(128)} %bitcast.27.me_ref, s32[1,1024]{1,0:T(1,128)} %bitcast.39, s32[1,128]{1,0:T(1,128)} %bitcast.41, s32[1,128]{1,0:T(1,128)} %bitcast.43, ...), custom_call_target="tpu_custom_call" | custom-call | tf_op jit(solution)/shard_map/pallas_call | solution.py:138
  5.7 117.9 %conditional.1 = (bf16[256,1024]{1,0:T(8,128)(2,1)S(1)}) conditional(s32[]{:T(128)} %bitcast.31, (s32[1024]{0:T(1024)}, s32[128]{0:T(128)}, s32[128]{0:T(128)}, s32[128,5]{0,1:T(8,128)}, s32[1]{0:T(128)}, /*index=5*/bf16[256,1024]{1,0:T(8,128)(2,1)}, bf16[8192]{0:T(1024)(128)(2,1)}, bf16[8192,1024]{1,0:T(8,128)(2,1)}, bf16[8192,128]{1,0:T(8,128)(2,1)}, ...), branch_computations={%region_0.1_spmd, %region_1.2_spmd} | conditional | flops 18119491584 | bytes 123485856 | solution.py:481
  6.0 0.0 copy-start.8
  6.0 7.3 %all-to-all-start.3 = ((bf16[16,56,1024]{2,1,0:T(8,128)(2,1)}), bf16[16,56,1024]{2,1,0:T(8,128)(2,1)S(1)}, u32[]{:S(2)}, u32[]{:S(2)}) async-start(bf16[16,56,1024]{2,1,0:T(8,128)(2,1)} %bitcast.38), calls=%async_computation.3 | async-start | bytes 3670016 | tf_op jit(solution)/shard_map/cond/branch_1_fun/all_to_all | solution.py:410
  13.3 0.0 copy-start.12
  13.4 0.2 multiply_reduce_fusion.1
  13.6 0.1 broadcast_in_dim.6
  13.6 0.1 reshape.88
  13.7 0.1 tile.12
  13.9 23.8 %all-to-all-done.3 = bf16[16,56,1024]{2,1,0:T(8,128)(2,1)S(1)} async-done(((bf16[16,56,1024]{2,1,0:T(8,128)(2,1)}), bf16[16,56,1024]{2,1,0:T(8,128)(2,1)S(1)}, u32[]{:S(2)}, u32[]{:S(2)}) %all-to-all-start.3) | async-done | bytes 1835040 | tf_op jit(solution)/shard_map/cond/branch_1_fun/all_to_all | solution.py:410
  37.6 0.0 copy-done.8
  37.6 1.4 %branch_1_fun.5 = (bf16[256,1024]{1,0:T(8,128)(2,1)S(1)}, f32[8,1,256]{2,1,0:T(1,128)}) custom-call(bf16[256,896]{1,0:T(8,128)(2,1)S(1)} %copy-done.8, bf16[896,1024]{1,0:T(8,128)(2,1)S(1)} %bitcast.33), custom_call_target="tpu_custom_call" | custom-call | tf_op jit(solution)/shard_map/cond/branch_1_fun/pallas_call | solution.py:186
  39.1 1.3 %collective-permute-start.8 = (bf16[256,1024]{1,0:T(8,128)(2,1)S(1)}, bf16[256,1024]{1,0:T(8,128)(2,1)S(1)}, u32[]{:S(2)}, u32[]{:S(2)}) collective-permute-start(bf16[256,1024]{1,0:T(8,128)(2,1)S(1)} %get-tuple-element.80.refs_0_), channel_id=1, source_target_pairs={{0,2},{1,3},{2,4},{3,5},{4,6},{5,7},{6,0},{7,1},{8,10},{9,11},{10,... | collective-permute-start | bytes 1572872 | tf_op jit(solution)/shard_map/cond/branch_1_fun/ppermute | solution.py:414
  40.4 1.4 %collective-permute-start.9 = (bf16[256,1024]{1,0:T(8,128)(2,1)S(1)}, bf16[256,1024]{1,0:T(8,128)(2,1)S(1)}, u32[]{:S(2)}, u32[]{:S(2)}) collective-permute-start(bf16[256,1024]{1,0:T(8,128)(2,1)S(1)} %get-tuple-element.80.refs_0_), channel_id=1, source_target_pairs={{0,6},{1,7},{2,0},{3,1},{4,2},{5,3},{6,4},{7,5},{8,14},{9,15},{10,... | collective-permute-start | bytes 1572872 | tf_op jit(solution)/shard_map/cond/branch_1_fun/ppermute | solution.py:414
  41.8 3.3 %collective-permute-start.10 = (bf16[256,1024]{1,0:T(8,128)(2,1)S(1)}, bf16[256,1024]{1,0:T(8,128)(2,1)S(1)}, u32[]{:S(2)}, u32[]{:S(2)}) collective-permute-start(bf16[256,1024]{1,0:T(8,128)(2,1)S(1)} %get-tuple-element.80.refs_0_), channel_id=1, source_target_pairs={{0,1},{1,0},{2,3},{3,2},{4,5},{5,4},{6,7},{7,6},{8,9},{9,8},{10,11... | collective-permute-start | bytes 1572872 | tf_op jit(solution)/shard_map/cond/branch_1_fun/ppermute | solution.py:414
  45.1 0.1 pad_add_fusion.3.order_ref
  45.2 0.5 fusion.1
  45.7 0.1 pad_maximum_fusion.2
  45.9 3.3 %all-to-all-start.4 = ((f32[8,1,256]{2,1,0:T(1,128)}), f32[8,1,256]{2,1,0:T(1,128)S(1)}, u32[]{:S(2)}, u32[]{:S(2)}) async-start(f32[8,1,256]{2,1,0:T(1,128)} %get-tuple-element.81), calls=%async_computation.4 | async-start | bytes 16384 | tf_op jit(solution)/shard_map/cond/branch_1_fun/all_to_all | solution.py:424
  49.2 0.1 pad_add_fusion.2.order_ref
  49.3 0.0 copy-done.12
  49.3 7.8 %all-to-all-done.4.sum_ref = f32[8,1,256]{2,1,0:T(1,128)S(1)} async-done(((f32[8,1,256]{2,1,0:T(1,128)}), f32[8,1,256]{2,1,0:T(1,128)S(1)}, u32[]{:S(2)}, u32[]{:S(2)}) %all-to-all-start.4) | async-done | bytes 8224 | tf_op jit(solution)/shard_map/cond/branch_1_fun/all_to_all | solution.py:424
  57.1 0.0 collective-permute-done.8.refs_1_
  57.1 0.0 collective-permute-done.9.refs_2_
  57.1 0.0 collective-permute-done.10.refs_3_
  57.1 0.6 collective-permute-start.11
  57.7 1.4 %collective-permute-start.13 = (bf16[256,1024]{1,0:T(8,128)(2,1)S(1)}, bf16[256,1024]{1,0:T(8,128)(2,1)S(1)}, u32[]{:S(2)}, u32[]{:S(2)}) collective-permute-start(bf16[256,1024]{1,0:T(8,128)(2,1)S(1)} %collective-permute-done.8.refs_1_), channel_id=1, source_target_pairs={{0,1},{1,0},{2,3},{3,2},{4,5},{5,4},{6,7},{7,6},{8,9},{9,8},{10,11... | collective-permute-start | bytes 1572872 | tf_op jit(solution)/shard_map/cond/branch_1_fun/ppermute | solution.py:414
  59.2 2.6 %collective-permute-start.12 = (bf16[256,1024]{1,0:T(8,128)(2,1)S(1)}, bf16[256,1024]{1,0:T(8,128)(2,1)S(1)}, u32[]{:S(2)}, u32[]{:S(2)}) collective-permute-start(bf16[256,1024]{1,0:T(8,128)(2,1)S(1)} %collective-permute-done.10.refs_3_), channel_id=1, source_target_pairs={{0,6},{1,7},{2,0},{3,1},{4,2},{5,3},{6,4},{7,5},{8,14},{9,15},{10,... | collective-permute-start | bytes 1572872 | tf_op jit(solution)/shard_map/cond/branch_1_fun/ppermute | solution.py:414
  61.7 0.0 copy-start.3
  61.7 0.0 copy-start.5
  61.7 8.0 %branch_1_fun.6.refs_7_ = f32[256,1280]{1,0:T(8,128)S(1)} custom-call(s32[4]{0:T(128)S(1)} %pad_add_fusion.2.order_ref, f32[8,1,256]{2,1,0:T(1,128)S(1)} %all-to-all-done.4.sum_ref, bf16[256,1024]{1,0:T(8,128)(2,1)S(1)} %get-tuple-element.80.refs_0_, bf16[256,1024]{1,0:T(8,128)(2,1)S(1)} %collective-permute-done.8.refs_1_, ...), custom_call_target="tpu_custom_call" | custom-call | flops 8053063680 | bytes 10485760 | tf_op jit(solution)/shard_map/cond/branch_1_fun/pallas_call | solution.py:246
  69.8 0.2 collective-permute-done.11.refs_0_
  70.0 0.3 collective-permute-done.12.refs_1_
  70.3 0.0 collective-permute-done.13.refs_2_
  70.3 0.9 collective-permute-start.14
  71.2 0.0 copy-start.7
  71.2 2.7 %collective-permute-start.15 = (bf16[128,1024]{1,0:T(8,128)(2,1)S(1)}, bf16[128,1024]{1,0:T(8,128)(2,1)S(1)}, u32[]{:S(2)}, u32[]{:S(2)}) collective-permute-start(bf16[128,1024]{1,0:T(8,128)(2,1)S(1)} %slice.16), channel_id=1, source_target_pairs={{0,6},{1,7},{2,0},{3,1},{4,2},{5,3},{6,4},{7,5},{8,14},{9,15},{10,... | collective-permute-start | bytes 786440 | tf_op jit(solution)/shard_map/cond/branch_1_fun/ppermute | solution.py:414
  73.9 0.0 copy-done.3
  73.9 0.0 copy-done.5
  73.9 6.0 %branch_1_fun.7.before_ref = f32[256,1280]{1,0:T(8,128)S(1)} custom-call(s32[3]{0:T(128)S(1)} %pad_add_fusion.3.order_ref, f32[8,1,256]{2,1,0:T(1,128)S(1)} %all-to-all-done.4.sum_ref, bf16[256,1024]{1,0:T(8,128)(2,1)S(1)} %collective-permute-done.11.refs_0_, bf16[256,1024]{1,0:T(8,128)(2,1)S(1)} %collective-permute-done.12.refs_1_, ...), custom_call_target="tpu_custom_call" | custom-call | flops 6039797760 | bytes 7864320 | tf_op jit(solution)/shard_map/cond/branch_1_fun/pallas_call | solution.py:246
  79.9 0.0 collective-permute-done.14.low_ref
  79.9 0.0 collective-permute-done.15.high_ref
  79.9 0.0 copy-done.7
  79.9 10.6 %branch_1_fun.8 = bf16[896,1024]{1,0:T(8,128)(2,1)S(1)} custom-call(s32[1]{0:T(128)} %bitcast.15.order_ref, s32[8,8]{1,0:T(8,128)S(1)} %get-tuple-element.77.info_ref, f32[8,1,256]{2,1,0:T(1,128)S(1)} %all-to-all-done.4.sum_ref, bf16[128,1024]{1,0:T(8,128)(2,1)S(1)} %collective-permute-done.14.low_ref, ...), custom_call_target="tpu_custom_call" | custom-call | flops 4026531840 | bytes 2621440 | tf_op jit(solution)/shard_map/cond/branch_1_fun/pallas_call | solution.py:369
  90.6 0.0 copy-start.10
  90.6 32.3 %all_to_all.25 = bf16[16,56,1024]{2,1,0:T(8,128)(2,1)S(1)} all-to-all(bf16[16,56,1024]{2,1,0:T(8,128)(2,1)S(1)} %bitcast.32), channel_id=1, replica_groups=mesh['sample'=16,'tensor'=8] {'sample'}, dimensions={0} | all-to-all | bytes 3670016 | tf_op jit(solution)/shard_map/cond/branch_1_fun/all_to_all | solution.py:451
  122.9 0.0 copy-done.10
  122.9 0.7 branch_1_fun.9
  123.6 0.0 copy-start.9
  123.6 0.8 copy-done.9
  (7 shorter events, 0.1 us)
Async XLA Ops:
  6.0 31.7 %copy-start.8 = (bf16[256,896]{1,0:T(8,128)(2,1)S(1)}, bf16[256,896]{1,0:T(8,128)(2,1)}, u32[]{:S(2)}) copy-start(bf16[256,896]{1,0:T(8,128)(2,1)} %get-tuple-element.78.hot_ref.back_ref) | copy-start | bytes 1376260 | tf_op jit(solution)/shard_map/cond
  6.0 31.7 %all-to-all-start.3 = ((bf16[16,56,1024]{2,1,0:T(8,128)(2,1)}), bf16[16,56,1024]{2,1,0:T(8,128)(2,1)S(1)}, u32[]{:S(2)}, u32[]{:S(2)}) async-start(bf16[16,56,1024]{2,1,0:T(8,128)(2,1)} %bitcast.38), calls=%async_computation.3 | async-start | bytes 3670016 | tf_op jit(solution)/shard_map/cond/branch_1_fun/all_to_all | solution.py:410
  13.3 36.0 %copy-start.12 = (bf16[8192]{0:T(1024)(128)(2,1)S(1)}, bf16[8192]{0:T(1024)(128)(2,1)}, u32[]{:S(2)}) copy-start(bf16[8192]{0:T(1024)(128)(2,1)} %get-tuple-element.86) | copy-start | bytes 49156 | tf_op jit(solution)/shard_map/cond
  39.1 18.0 %collective-permute-start.8 = (bf16[256,1024]{1,0:T(8,128)(2,1)S(1)}, bf16[256,1024]{1,0:T(8,128)(2,1)S(1)}, u32[]{:S(2)}, u32[]{:S(2)}) collective-permute-start(bf16[256,1024]{1,0:T(8,128)(2,1)S(1)} %get-tuple-element.80.refs_0_), channel_id=1, source_target_pairs={{0,2},{1,3},{2,4},{3,5},{4,6},{5,7},{6,0},{7,1},{8,10},{9,11},{10,... | collective-permute-start | bytes 1572872 | tf_op jit(solution)/shard_map/cond/branch_1_fun/ppermute | solution.py:414
  40.4 16.7 %collective-permute-start.9 = (bf16[256,1024]{1,0:T(8,128)(2,1)S(1)}, bf16[256,1024]{1,0:T(8,128)(2,1)S(1)}, u32[]{:S(2)}, u32[]{:S(2)}) collective-permute-start(bf16[256,1024]{1,0:T(8,128)(2,1)S(1)} %get-tuple-element.80.refs_0_), channel_id=1, source_target_pairs={{0,6},{1,7},{2,0},{3,1},{4,2},{5,3},{6,4},{7,5},{8,14},{9,15},{10,... | collective-permute-start | bytes 1572872 | tf_op jit(solution)/shard_map/cond/branch_1_fun/ppermute | solution.py:414
  41.8 15.3 %collective-permute-start.10 = (bf16[256,1024]{1,0:T(8,128)(2,1)S(1)}, bf16[256,1024]{1,0:T(8,128)(2,1)S(1)}, u32[]{:S(2)}, u32[]{:S(2)}) collective-permute-start(bf16[256,1024]{1,0:T(8,128)(2,1)S(1)} %get-tuple-element.80.refs_0_), channel_id=1, source_target_pairs={{0,1},{1,0},{2,3},{3,2},{4,5},{5,4},{6,7},{7,6},{8,9},{9,8},{10,11... | collective-permute-start | bytes 1572872 | tf_op jit(solution)/shard_map/cond/branch_1_fun/ppermute | solution.py:414
  45.9 11.2 %all-to-all-start.4 = ((f32[8,1,256]{2,1,0:T(1,128)}), f32[8,1,256]{2,1,0:T(1,128)S(1)}, u32[]{:S(2)}, u32[]{:S(2)}) async-start(f32[8,1,256]{2,1,0:T(1,128)} %get-tuple-element.81), calls=%async_computation.4 | async-start | bytes 16384 | tf_op jit(solution)/shard_map/cond/branch_1_fun/all_to_all | solution.py:424
  57.1 12.8 %collective-permute-start.11 = (bf16[256,1024]{1,0:T(8,128)(2,1)S(1)}, bf16[256,1024]{1,0:T(8,128)(2,1)S(1)}, u32[]{:S(2)}, u32[]{:S(2)}) collective-permute-start(bf16[256,1024]{1,0:T(8,128)(2,1)S(1)} %collective-permute-done.8.refs_1_), channel_id=1, source_target_pairs={{0,2},{1,3},{2,4},{3,5},{4,6},{5,7},{6,0},{7,1},{8,10},{9,11},{10,... | collective-permute-start | bytes 1572872 | tf_op jit(solution)/shard_map/cond/branch_1_fun/ppermute | solution.py:414
  57.7 12.6 %collective-permute-start.13 = (bf16[256,1024]{1,0:T(8,128)(2,1)S(1)}, bf16[256,1024]{1,0:T(8,128)(2,1)S(1)}, u32[]{:S(2)}, u32[]{:S(2)}) collective-permute-start(bf16[256,1024]{1,0:T(8,128)(2,1)S(1)} %collective-permute-done.8.refs_1_), channel_id=1, source_target_pairs={{0,1},{1,0},{2,3},{3,2},{4,5},{5,4},{6,7},{7,6},{8,9},{9,8},{10,11... | collective-permute-start | bytes 1572872 | tf_op jit(solution)/shard_map/cond/branch_1_fun/ppermute | solution.py:414
  59.2 11.1 %collective-permute-start.12 = (bf16[256,1024]{1,0:T(8,128)(2,1)S(1)}, bf16[256,1024]{1,0:T(8,128)(2,1)S(1)}, u32[]{:S(2)}, u32[]{:S(2)}) collective-permute-start(bf16[256,1024]{1,0:T(8,128)(2,1)S(1)} %collective-permute-done.10.refs_3_), channel_id=1, source_target_pairs={{0,6},{1,7},{2,0},{3,1},{4,2},{5,3},{6,4},{7,5},{8,14},{9,15},{10,... | collective-permute-start | bytes 1572872 | tf_op jit(solution)/shard_map/cond/branch_1_fun/ppermute | solution.py:414
  61.7 12.2 %copy-start.3 = (bf16[8192,128]{1,0:T(8,128)(2,1)S(1)}, bf16[8192,128]{1,0:T(8,128)(2,1)}, u32[]{:S(2)}) copy-start(bf16[8192,128]{1,0:T(8,128)(2,1)} %get-tuple-element.88.refs_6_.refs_5_.wk_ref) | copy-start | bytes 6291460 | tf_op jit(solution)/shard_map/cond
  61.7 12.2 %copy-start.5 = (bf16[8192,128]{1,0:T(8,128)(2,1)S(1)}, bf16[8192,128]{1,0:T(8,128)(2,1)}, u32[]{:S(2)}) copy-start(bf16[8192,128]{1,0:T(8,128)(2,1)} %get-tuple-element.89.refs_7_.refs_6_.wv_ref) | copy-start | bytes 6291460 | tf_op jit(solution)/shard_map/cond
  70.3 9.6 %collective-permute-start.14 = (bf16[128,1024]{1,0:T(8,128)(2,1)S(1)}, bf16[128,1024]{1,0:T(8,128)(2,1)S(1)}, u32[]{:S(2)}, u32[]{:S(2)}) collective-permute-start(bf16[128,1024]{1,0:T(8,128)(2,1)S(1)} %slice.15), channel_id=1, source_target_pairs={{0,2},{1,3},{2,4},{3,5},{4,6},{5,7},{6,0},{7,1},{8,10},{9,11},{10,... | collective-permute-start | bytes 786440 | tf_op jit(solution)/shard_map/cond/branch_1_fun/ppermute | solution.py:414
  71.2 8.7 %copy-start.7 = (bf16[40,2,128,128]{3,2,1,0:T(8,128)(2,1)S(1)}, bf16[40,2,128,128]{3,2,1,0:T(8,128)(2,1)}, u32[]{:S(2)}) copy-start(bf16[40,2,128,128]{3,2,1,0:T(8,128)(2,1)} %get-tuple-element.97.pool_ref) | copy-start | bytes 7864324 | tf_op jit(solution)/shard_map/cond
  71.2 8.7 %collective-permute-start.15 = (bf16[128,1024]{1,0:T(8,128)(2,1)S(1)}, bf16[128,1024]{1,0:T(8,128)(2,1)S(1)}, u32[]{:S(2)}, u32[]{:S(2)}) collective-permute-start(bf16[128,1024]{1,0:T(8,128)(2,1)S(1)} %slice.16), channel_id=1, source_target_pairs={{0,6},{1,7},{2,0},{3,1},{4,2},{5,3},{6,4},{7,5},{8,14},{9,15},{10,... | collective-permute-start | bytes 786440 | tf_op jit(solution)/shard_map/cond/branch_1_fun/ppermute | solution.py:414
  90.6 32.3 %copy-start.10 = (bf16[896,256]{1,0:T(8,128)(2,1)S(1)}, bf16[896,256]{1,0:T(8,128)(2,1)}, u32[]{:S(2)}) copy-start(bf16[896,256]{1,0:T(8,128)(2,1)} %get-tuple-element.76.hot_ref) | copy-start | bytes 1376260 | tf_op jit(solution)/shard_map/cond
  123.6 0.8 copy-start.9
